TPU v7x, 32 devices: a whole 2x2x4 slice. The times are simulated.
32 devices in a mesh: dp: 2 (over x), expert: 16 (over z, y, core).
Axes of the slice: x: 2, y: 2, z: 4, core: 2. Of those that a mesh axis runs over, the one named last changes fastest.
Arguments:
- tokens: bfloat16 [768, 1024], P(('dp', 'expert')), may hold values from -6 to 6
- grad_out: bfloat16 [768, 1024], P(('dp', 'expert')), may hold values from -6 to 6
- expert_ids: int32 [768, 8], P(('dp', 'expert')), may hold values from 0 to 15, all different within a row; in each aligned block of 24 rows (0 to 23, 24 to 47, ...) at most 18 rows name the same one
- gates: float32 [768, 8], P(('dp', 'expert')), may hold values from 0.05 to 0.5
- w_in: bfloat16 [16, 1024, 2, 512], P('expert', None, None, 'dp'), may hold values from -0.1875 to 0.1875
- w_out: bfloat16 [16, 512, 1024], P('expert', 'dp'), may hold values from -0.25 to 0.25
Outputs:
- mixed: bfloat16 [768, 1024], P(('dp', 'expert'))
- grad_tokens: bfloat16 [768, 1024], P(('dp', 'expert'))
- grad_gates: float32 [768, 8], P(('dp', 'expert'))
- grad_w_in: float32 [16, 1024, 2, 512], P('expert', None, None, 'dp')
- grad_w_out: float32 [16, 512, 1024], P('expert', 'dp')
Inputs may be any that keep to these rules, and one draw needn't show every extreme that they name: `expert_ids`: each token names 8 different experts; the rows of one device name no expert more than 18 times, a bound that some block reaches.
All inputs are finite; a program needn't handle non-finite values.
Results may differ from a plain program's by a relative error of at most 0.012.
Values may be sent and summed in bfloat16 or wider, within the bound.
A program may use at most 64 MiB of HBM per device.

v0:
```python
import jax
import jax.numpy as jnp
from jax import lax
from jax.sharding import PartitionSpec as P


def forward_part(rows, weight_in, weight_out):
    model_width = rows.shape[1]
    hidden_width = weight_out.shape[0]
    flat_in = weight_in.reshape(model_width, 2 * hidden_width)
    preact = jnp.dot(rows, flat_in, preferred_element_type=jnp.float32)
    gate_part = preact[:, :hidden_width]
    up_part = preact[:, hidden_width:]
    activated = gate_part * jax.nn.sigmoid(gate_part)
    hidden = (activated * up_part).astype(jnp.bfloat16)
    result = jnp.dot(hidden, weight_out, preferred_element_type=jnp.float32).astype(jnp.bfloat16)
    return (preact, hidden, result)


def backward_part(rows, preact, hidden, grad_rows, weight_in, weight_out):
    model_width = rows.shape[1]
    hidden_width = weight_out.shape[0]
    flat_in = weight_in.reshape(model_width, 2 * hidden_width)
    gate_part = preact[:, :hidden_width]
    up_part = preact[:, hidden_width:]
    sigmoid_gate = jax.nn.sigmoid(gate_part)
    activated = gate_part * sigmoid_gate
    back_grad = jnp.einsum("sd,hd->sh", grad_rows, weight_out, preferred_element_type=jnp.float32)
    grad_gate = back_grad * up_part * (sigmoid_gate * (1.0 + gate_part * (1.0 - sigmoid_gate)))
    grad_up = back_grad * activated
    grad_pre = jnp.concatenate([grad_gate, grad_up], axis=1).astype(jnp.bfloat16)
    grad_rows_in = jnp.einsum(
        "sk,dk->sd", grad_pre, flat_in, preferred_element_type=jnp.float32
    ).astype(jnp.bfloat16)
    grad_weight_in = jnp.einsum("sd,sk->dk", rows, grad_pre, preferred_element_type=jnp.float32)
    grad_weight_out = jnp.einsum("sh,sd->hd", hidden, grad_rows, preferred_element_type=jnp.float32)
    return (grad_rows_in, grad_weight_in, grad_weight_out)


def per_device(tokens, grad_out, expert_ids, gates, w_in, w_out):
    count_tok, model_width = tokens.shape
    per_token = expert_ids.shape[1]
    groups = lax.axis_size("expert")
    capacity = min(count_tok, 3 * count_tok * per_token // (2 * groups))
    row_count = count_tok * per_token
    flat_ids = expert_ids.reshape(-1)
    onehot = (flat_ids[:, None] == jnp.arange(groups, dtype=jnp.int32)[None, :]).astype(jnp.int32)
    order_rank = jnp.sum((jnp.cumsum(onehot, axis=0) - onehot) * onehot, axis=1)
    slot_of_row = flat_ids * capacity + order_rank
    inverse = (
        jnp.full((groups * capacity,), row_count, jnp.int32)
        .at[slot_of_row]
        .set(jnp.arange(row_count, dtype=jnp.int32))
    )
    token_of_slot = jnp.where(inverse < row_count, inverse // per_token, count_tok)
    tokens_padded = jnp.concatenate([tokens, jnp.zeros((1, model_width), jnp.bfloat16)], axis=0)
    grad_padded = jnp.concatenate([grad_out, jnp.zeros((1, model_width), jnp.bfloat16)], axis=0)
    gates_padded = jnp.concatenate([gates.reshape(-1), jnp.zeros((1,), jnp.float32)], axis=0)
    send_rows = tokens_padded[token_of_slot].reshape(groups, capacity, model_width)
    slot_gate = gates_padded[inverse]
    send_grads = (slot_gate[:, None] * grad_padded[token_of_slot].astype(jnp.float32)).astype(
        jnp.bfloat16
    )
    send_grads = send_grads.reshape(groups, capacity, model_width)
    full_in, full_out = (
        lax.all_gather(w_in, "dp", axis=3, tiled=True),
        lax.all_gather(w_out, "dp", axis=1, tiled=True),
    )
    weight_in = full_in[0]
    weight_out = full_out[0]
    hidden_width = weight_out.shape[0]
    arrived_rows = lax.all_to_all(send_rows, "expert", split_axis=0, concat_axis=0, tiled=True)
    rows = arrived_rows.reshape(groups * capacity, model_width)
    preact, hidden, result = forward_part(rows, weight_in, weight_out)
    back_out = lax.all_to_all(
        result.reshape(groups, capacity, model_width),
        "expert",
        split_axis=0,
        concat_axis=0,
        tiled=True,
    )
    arrived_grads = lax.all_to_all(send_grads, "expert", split_axis=0, concat_axis=0, tiled=True)
    grad_rows = arrived_grads.reshape(groups * capacity, model_width)
    grad_rows_in, grad_weight_in, grad_weight_out = backward_part(
        rows, preact, hidden, grad_rows, weight_in, weight_out
    )
    back_grads = lax.all_to_all(
        grad_rows_in.reshape(groups, capacity, model_width),
        "expert",
        split_axis=0,
        concat_axis=0,
        tiled=True,
    )
    out_rows = back_out.reshape(groups * capacity, model_width)[slot_of_row].reshape(
        count_tok, per_token, model_width
    )
    mixed = jnp.sum(gates[:, :, None] * out_rows.astype(jnp.float32), axis=1).astype(jnp.bfloat16)
    grad_gates = jnp.einsum("td,tkd->tk", grad_out, out_rows, preferred_element_type=jnp.float32)
    route_dx = back_grads.reshape(groups * capacity, model_width)[slot_of_row].reshape(
        count_tok, per_token, model_width
    )
    grad_tokens = jnp.sum(route_dx.astype(jnp.float32), axis=1).astype(jnp.bfloat16)
    grad_in_shard, grad_out_shard = (
        lax.psum_scatter(
            grad_weight_in.reshape(1, model_width, 2, hidden_width).astype(jnp.bfloat16),
            "dp",
            scatter_dimension=3,
            tiled=True,
        ).astype(jnp.float32),
        lax.psum_scatter(
            grad_weight_out[None].astype(jnp.bfloat16), "dp", scatter_dimension=1, tiled=True
        ).astype(jnp.float32),
    )
    return (mixed, grad_tokens, grad_gates, grad_in_shard, grad_out_shard)


def solution(mesh):
    in_specs = (
        P(("dp", "expert"), None),
        P(("dp", "expert"), None),
        P(("dp", "expert"), None),
        P(("dp", "expert"), None),
        P("expert", None, None, "dp"),
        P("expert", "dp", None),
    )
    out_specs = (
        P(("dp", "expert"), None),
        P(("dp", "expert"), None),
        P(("dp", "expert"), None),
        P("expert", None, None, "dp"),
        P("expert", "dp", None),
    )
    return jax.shard_map(
        per_device, mesh=mesh, in_specs=in_specs, out_specs=out_specs, check_vma=False
    )
```

profile of v0, /device:TPU:0, one launch (start us, length us, event | category | flops | bytes accessed | tf_op | source)
XLA Modules:
  0.0 150.4 jit_solution(11360080915823369887)
XLA Ops:
  7.2 0.0 all-gather.3.cloned.1.call-start
  7.2 0.7 all-gather.3.cloned.1.call-update
  7.9 0.7 broadcast_multiply_fusion
  8.6 0.8 copy.16
  9.3 0.1 eq.22
  9.5 0.6 reduce-window.6
  10.1 0.2 slice_reduce_fusion
  10.3 0.1 bitcast_bitcast_fusion
  10.4 0.1 copy.15
  10.5 0.1 mul.63
  10.6 0.8 concatenate.13
  11.4 1.2 scatter_custom_fusion
  12.6 2.1 %gather_fusion = bf16[288,1024]{1,0:T(8,128)(2,1)S(1)} fusion(bf16[25,1024]{1,0:T(8,128)(2,1)S(1)} %concatenate.13, s32[1024]{0:T(1024)S(1)} %get-tuple-element.21), kind=kCustom, calls=%fused_computation | custom fusion | bytes 1180800 | tf_op jit(solution)/shard_map/gather | solution.py:59
  14.7 1.1 reshape.99
  15.8 7.4 %all-to-all-start = ((bf16[16,18,1024]{2,1,0:T(8,128)(2,1)}), bf16[16,18,1024]{2,1,0:T(8,128)(2,1)S(1)}, u32[]{:S(2)}, u32[]{:S(2)}) async-start(bf16[16,18,1024]{2,1,0:T(8,128)(2,1)} %reshape.99), calls=%async_computation | async-start | bytes 1572864 | tf_op jit(solution)/shard_map/all_to_all | solution.py:72
  23.2 2.1 %gather_fusion.3 = bf16[288,1024]{1,0:T(8,128)(2,1)S(1)} fusion(bf16[25,1024]{1,0:T(8,128)(2,1)S(1)} %concatenate.15, s32[1024]{0:T(1024)S(1)} %get-tuple-element.21), kind=kCustom, calls=%fused_computation.3 | custom fusion | bytes 1180800 | tf_op jit(solution)/shard_map/gather | solution.py:61
  25.3 0.1 reshape.110
  25.4 0.5 copy-done.4
  25.9 0.1 copy.14
  26.0 0.1 reshape.104
  26.1 0.1 pad_maximum_fusion.1
  26.2 2.5 %gather_fusion.2 = f32[288]{0:T(512)S(1)} fusion(f32[193]{0:T(256)S(1)} %pad_maximum_fusion.1, s32[1024]{0:T(1024)S(1)} %get-tuple-element.20), kind=kCustom, calls=%fused_computation.2 | custom fusion | bytes 3456 | tf_op jit(solution)/shard_map/gather | solution.py:60
  28.6 0.1 mul.68
  28.7 1.0 multiply_convert_fusion
  29.8 12.1 %all-to-all-done = bf16[16,18,1024]{2,1,0:T(8,128)(2,1)S(1)} async-done(((bf16[16,18,1024]{2,1,0:T(8,128)(2,1)}), bf16[16,18,1024]{2,1,0:T(8,128)(2,1)S(1)}, u32[]{:S(2)}, u32[]{:S(2)}) %all-to-all-start) | async-done | bytes 589856 | tf_op jit(solution)/shard_map/all_to_all | solution.py:72
  41.9 5.5 %all-to-all-start.2 = ((bf16[16,18,1024]{2,1,0:T(8,128)(2,1)}), bf16[16,18,1024]{2,1,0:T(8,128)(2,1)S(1)}, u32[]{:S(2)}, u32[]{:S(2)}) async-start(bf16[16,18,1024]{2,1,0:T(8,128)(2,1)} %multiply_convert_fusion), calls=%async_computation.2 | async-start | bytes 1572864 | tf_op jit(solution)/shard_map/all_to_all | solution.py:82
  47.3 0.0 all-gather.5.cloned.1.call-start
  47.4 0.7 all-gather.5.cloned.1.call-update
  48.1 0.0 reduce-scatter.5.cloned.1.call-start
  48.1 1.0 reshape.100
  49.1 16.9 %all-to-all-done.2 = bf16[16,18,1024]{2,1,0:T(8,128)(2,1)S(1)} async-done(((bf16[16,18,1024]{2,1,0:T(8,128)(2,1)}), bf16[16,18,1024]{2,1,0:T(8,128)(2,1)S(1)}, u32[]{:S(2)}, u32[]{:S(2)}) %all-to-all-start.2) | async-done | bytes 589856 | tf_op jit(solution)/shard_map/all_to_all | solution.py:82
  66.0 0.2 reshape.105
  66.2 0.0 all-gather.3.cloned.1.call-done
  66.3 2.2 %copy.27 = bf16[128,8,2,512]{3,1,2,0:T(8,128)(2,1)S(1)} copy(bf16[128,8,2,512]{3,2,1,0:T(2,128)(2,1)} %bitcast.49) | data formatting | bytes 4194304
  68.5 1.8 %fusion.17 = f32[288,1024]{1,0:T(8,128)} fusion(bf16[288,1024]{1,0:T(8,128)(2,1)S(1)} %copy-done, bf16[1024,1024]{1,0:T(8,128)(2,1)S(1)} %bitcast.50), kind=kOutput, calls=%fused_computation.56 | convolution fusion | flops 603979776 | bytes 3866624 | tf_op jit(solution)/shard_map/dot_general | solution.py:11
  70.3 2.1 %all-gather.5.cloned.1.call-done = bf16[1,512,1024]{2,1,0:T(8,128)(2,1)} async-done(((bf16[1,256,1024]{2,1,0:T(8,128)(2,1)}), bf16[1,512,1024]{2,1,0:T(8,128)(2,1)}) %all-gather.5.cloned.1.call-update) | async-done | bytes 1048592 | tf_op jit(solution)/shard_map/all_gather | solution.py:67
  72.4 3.0 %multiply_convert_fusion.2 = (bf16[288,512]{1,0:T(8,128)(2,1)}, bf16[288,512]{1,0:T(8,128)(2,1)}, bf16[288,512]{1,0:T(8,128)(2,1)S(1)}) fusion(f32[288,1024]{1,0:T(8,128)} %fusion.17, bf16[288,1024]{1,0:T(8,128)(2,1)S(1)} %reshape.105, bf16[1,512,1024]{2,1,0:T(8,128)(2,1)} %all-gather.5.cloned.1.call-done), kind=kOutput, calls=%fused_computation.20 | convolution fusion | flops 304201728 | bytes 3702784 | tf_op jit(solution)/shard_map/sd,hd->sh/dot_general | solution.py:28
  75.4 0.7 copy-done.1
  76.1 1.7 %fusion = bf16[1,512,1024]{2,1,0:T(8,128)(2,1)} fusion(bf16[288,512]{1,0:T(8,128)(2,1)S(1)} %get-tuple-element.17, bf16[288,1024]{1,0:T(8,128)(2,1)S(1)} %reshape.105), kind=kOutput, calls=%fused_computation.9 | convolution fusion | flops 302514176 | bytes 1933312 | tf_op jit(solution)/shard_map/sh,sd->hd/dot_general | solution.py:36
  77.8 0.0 reduce-scatter.5.cloned.1.call-update
  77.9 0.0 reduce-scatter.3.cloned.1.call-start
  77.9 0.2 reshape.164
  78.1 1.1 pad_maximum_fusion
  79.2 2.6 %convert_bitcast_fusion = bf16[1,1024,2,512]{3,1,2,0:T(8,128)(2,1)} fusion(bf16[288,1024,1]{1,0,2:T(8,128)(2,1)S(1)} %reshape.164, bf16[36,2,8,512]{3,2,1,0:T(8,128)(2,1)S(1)} %bitcast.52), kind=kOutput, calls=%fused_computation.6 | convolution fusion | flops 605028352 | bytes 3276800 | tf_op jit(solution)/shard_map/sd,sk->dk/dot_general | solution.py:35
  81.8 0.0 reduce-scatter.3.cloned.1.call-update
  81.9 0.9 copy-done.2
  82.8 1.8 %convolution_convert_fusion.2 = bf16[288,1024]{1,0:T(8,128)(2,1)S(1)} fusion(bf16[288,512]{1,0:T(8,128)(2,1)S(1)} %copy-done.2, bf16[1,512,1024]{2,1,0:T(8,128)(2,1)} %all-gather.5.cloned.1.call-done), kind=kOutput, calls=%fused_computation.11 | convolution fusion | flops 302284800 | bytes 1933312 | tf_op jit(solution)/shard_map/dot_general | solution.py:16
  84.6 1.1 reshape.101
  85.6 5.6 %all-to-all-start.1 = ((bf16[16,18,1024]{2,1,0:T(8,128)(2,1)}), bf16[16,18,1024]{2,1,0:T(8,128)(2,1)S(1)}, u32[]{:S(2)}, u32[]{:S(2)}) async-start(bf16[16,18,1024]{2,1,0:T(8,128)(2,1)} %reshape.101), calls=%async_computation.1 | async-start | bytes 1572864 | tf_op jit(solution)/shard_map/all_to_all | solution.py:75
  91.2 1.9 %convolution_convert_fusion.1 = bf16[288,1024]{1,0:T(8,128)(2,1)S(1)} fusion(bf16[1024,1024]{1,0:T(8,128)(2,1)S(1)} %bitcast.51, bf16[288,512]{1,0:T(8,128)(2,1)} %get-tuple-element.16, bf16[288,512]{1,0:T(8,128)(2,1)} %get-tuple-element.15), kind=kOutput, calls=%fused_computation.10 | convolution fusion | flops 605454336 | bytes 3276800 | tf_op jit(solution)/shard_map/sk,dk->sd/dot_general | solution.py:32
  93.1 1.1 reshape.106
  94.1 15.8 %all-to-all-done.1 = bf16[16,18,1024]{2,1,0:T(8,128)(2,1)S(1)} async-done(((bf16[16,18,1024]{2,1,0:T(8,128)(2,1)}), bf16[16,18,1024]{2,1,0:T(8,128)(2,1)S(1)}, u32[]{:S(2)}, u32[]{:S(2)}) %all-to-all-start.1) | async-done | bytes 589856 | tf_op jit(solution)/shard_map/all_to_all | solution.py:75
  109.9 5.5 %all-to-all-start.3 = ((bf16[16,18,1024]{2,1,0:T(8,128)(2,1)}), bf16[16,18,1024]{2,1,0:T(8,128)(2,1)S(1)}, u32[]{:S(2)}, u32[]{:S(2)}) async-start(bf16[16,18,1024]{2,1,0:T(8,128)(2,1)} %reshape.106), calls=%async_computation.3 | async-start | bytes 1572864 | tf_op jit(solution)/shard_map/all_to_all | solution.py:87
  115.4 0.2 reshape.102
  115.6 1.0 gather_fusion.1
  116.6 17.5 %all-to-all-done.3 = bf16[16,18,1024]{2,1,0:T(8,128)(2,1)S(1)} async-done(((bf16[16,18,1024]{2,1,0:T(8,128)(2,1)}), bf16[16,18,1024]{2,1,0:T(8,128)(2,1)S(1)}, u32[]{:S(2)}, u32[]{:S(2)}) %all-to-all-start.3) | async-done | bytes 589856 | tf_op jit(solution)/shard_map/all_to_all | solution.py:87
  134.1 0.2 reshape.107
  134.3 1.0 gather_fusion.4
  135.3 0.3 fusion.7
  135.6 0.7 copy.23
  136.3 0.9 bitcast_reduce_fusion
  137.2 0.9 multiply_reduce_fusion
  138.1 2.1 %convert_element_type.65 = f32[1,256,1024]{2,1,0:T(8,128)} convert(bf16[1,256,1024]{2,1,0:T(8,128)(2,1)} %reduce-scatter.5.cloned.1.call-done) | non-fusion elementwise | flops 262144 | bytes 1572864 | tf_op jit(solution)/shard_map/convert_element_type | solution.py:112
  140.2 3.6 %copy.21 = f32[1,1024,2,256]{3,2,1,0:T(2,128)} copy(bf16[1,1024,2,256]{3,1,2,0:T(8,128)(2,1)} %reduce-scatter.3.cloned.1.call-done) | data formatting | bytes 3145728
  (20 shorter events, 0.1 us)
Async XLA Ops:
  7.2 59.1 %all-gather.3.cloned.1.call-start = ((), (), s32[]{:S(2)}) async-start(), calls=%async_computation.6 | async-start | bytes 3145728 | tf_op jit(solution)/shard_map/all_gather | solution.py:66
  14.7 8.5 %copy-start.3 = (bf16[24,1024]{1,0:T(8,128)(2,1)S(1)}, bf16[24,1024]{1,0:T(8,128)(2,1)}, u32[]{:S(2)}) copy-start(bf16[24,1024]{1,0:T(8,128)(2,1)} %param.7) | copy-start | bytes 147460
  15.8 26.1 %all-to-all-start = ((bf16[16,18,1024]{2,1,0:T(8,128)(2,1)}), bf16[16,18,1024]{2,1,0:T(8,128)(2,1)S(1)}, u32[]{:S(2)}, u32[]{:S(2)}) async-start(bf16[16,18,1024]{2,1,0:T(8,128)(2,1)} %reshape.99), calls=%async_computation | async-start | bytes 1572864 | tf_op jit(solution)/shard_map/all_to_all | solution.py:72
  25.3 0.7 copy-start.4
  41.9 24.2 %all-to-all-start.2 = ((bf16[16,18,1024]{2,1,0:T(8,128)(2,1)}), bf16[16,18,1024]{2,1,0:T(8,128)(2,1)S(1)}, u32[]{:S(2)}, u32[]{:S(2)}) async-start(bf16[16,18,1024]{2,1,0:T(8,128)(2,1)} %multiply_convert_fusion), calls=%async_computation.2 | async-start | bytes 1572864 | tf_op jit(solution)/shard_map/all_to_all | solution.py:82
  47.3 25.0 %all-gather.5.cloned.1.call-start = ((), (), s32[]{:S(2)}) async-start(), calls=%async_computation.7 | async-start | bytes 1572864 | tf_op jit(solution)/shard_map/all_gather | solution.py:67
  48.1 90.0 %reduce-scatter.5.cloned.1.call-start = ((), (), s32[]{:S(2)}) async-start(), calls=%async_computation.9 | async-start | bytes 1572864 | tf_op jit(solution)/shard_map/reduce_scatter | solution.py:110
  66.3 2.2 %copy-start = (bf16[288,1024]{1,0:T(8,128)(2,1)S(1)}, bf16[288,1024]{1,0:T(8,128)(2,1)}, u32[]{:S(2)}) copy-start(bf16[288,1024]{1,0:T(8,128)(2,1)} %reshape.100) | copy-start | bytes 1769476
  75.4 0.7 copy-start.1
  77.9 62.4 %reduce-scatter.3.cloned.1.call-start = ((), (), s32[]{:S(2)}) async-start(), calls=%async_computation.8 | async-start | bytes 3145728 | tf_op jit(solution)/shard_map/reduce_scatter | solution.py:104
  81.8 1.0 copy-start.2
  85.6 24.3 %all-to-all-start.1 = ((bf16[16,18,1024]{2,1,0:T(8,128)(2,1)}), bf16[16,18,1024]{2,1,0:T(8,128)(2,1)S(1)}, u32[]{:S(2)}, u32[]{:S(2)}) async-start(bf16[16,18,1024]{2,1,0:T(8,128)(2,1)} %reshape.101), calls=%async_computation.1 | async-start | bytes 1572864 | tf_op jit(solution)/shard_map/all_to_all | solution.py:75
  109.9 24.2 %all-to-all-start.3 = ((bf16[16,18,1024]{2,1,0:T(8,128)(2,1)}), bf16[16,18,1024]{2,1,0:T(8,128)(2,1)S(1)}, u32[]{:S(2)}, u32[]{:S(2)}) async-start(bf16[16,18,1024]{2,1,0:T(8,128)(2,1)} %reshape.106), calls=%async_computation.3 | async-start | bytes 1572864 | tf_op jit(solution)/shard_map/all_to_all | solution.py:87
Sparse Core Ops, SparseCore 0:
  9.5 35.7 all-gather.2
  49.7 22.6 all-gather.4
  78.0 20.3 reduce-scatter.4
  101.1 31.8 reduce-scatter.2
where the time goes:
time: 151 us; the launch traced here: 150 us
  waiting for transfers between devices  65.8 us (44%)
  local copies, waits for them, and re-layouts  25.8 us (17%)
  starting transfers between devices  24.1 us (16%)
  between operations  14 us (9%)
  matrix products  13.1 us (9%)
  other arithmetic  7.6 us (5%)
    all_to_all x1, waiting for transfers between devices, per_device(): lax.all_to_all(grad_rows_in.reshape(groups, capacity, model_width), 'expe...  17.5 us
    all_to_all x1, waiting for transfers between devices, per_device(): lax.all_to_all(send_grads, 'expert', split_axis=0, concat_axis=0, tiled=T...  16.9 us
    all_to_all x1, waiting for transfers between devices, per_device(): lax.all_to_all(result.reshape(groups, capacity, model_width), 'expert', s...  15.8 us
    all_to_all x1, waiting for transfers between devices, per_device(): lax.all_to_all(send_rows, 'expert', split_axis=0, concat_axis=0, tiled=True)  12.1 us
    unnamed x14, local copies, waits for them, and re-layouts  8.85 us
    all_to_all x1, starting transfers between devices, per_device(): lax.all_to_all(send_rows, 'expert', split_axis=0, concat_axis=0, tiled=True)  7.39 us
    all_to_all x1, starting transfers between devices, per_device(): lax.all_to_all(result.reshape(groups, capacity, model_width), 'expert', s...  5.56 us
    all_to_all x1, starting transfers between devices, per_device(): lax.all_to_all(grad_rows_in.reshape(groups, capacity, model_width), 'expe...  5.48 us
  transfers between devices with their start and end apart: 8, of which 5 were waited for; matrix products, arithmetic and copies ran while one was open for 24% of the time, Pallas kernels for 0%

commit v1 on v0

--- a/solution.py
+++ b/solution.py
@@ -37,7 +37,7 @@
     return (grad_rows_in, grad_weight_in, grad_weight_out)
 
 
-def per_device(tokens, grad_out, expert_ids, gates, w_in, w_out):
+def routed_plan(tokens, grad_out, expert_ids, gates, w_in, w_out):
     count_tok, model_width = tokens.shape
     per_token = expert_ids.shape[1]
     groups = lax.axis_size("expert")
@@ -114,6 +114,86 @@
     return (mixed, grad_tokens, grad_gates, grad_in_shard, grad_out_shard)
 
 
+def expert_math(rows, cotangent, gate, weight_in, weight_out):
+    half = weight_out.shape[0]
+    preact = jnp.dot(rows, weight_in, preferred_element_type=jnp.float32)
+    gate_part = preact[:, :half]
+    up_part = preact[:, half:]
+    sig = jax.nn.sigmoid(gate_part)
+    activated = gate_part * sig
+    hidden = activated * up_part
+    back = jnp.einsum("sd,hd->sh", cotangent, weight_out, preferred_element_type=jnp.float32)
+    gate_grad = jnp.sum(hidden * back, axis=1, keepdims=True)
+    gated_hidden = (gate * hidden).astype(jnp.bfloat16)
+    gated_back = gate * back
+    grad_gate = gated_back * up_part * (sig * (1.0 + gate_part * (1.0 - sig)))
+    grad_up = gated_back * activated
+    grad_pre = jnp.concatenate([grad_gate, grad_up], axis=1).astype(jnp.bfloat16)
+    mixed = jnp.dot(gated_hidden, weight_out, preferred_element_type=jnp.float32)
+    grad_rows = jnp.einsum("sk,dk->sd", grad_pre, weight_in, preferred_element_type=jnp.float32)
+    grad_weight_in = jnp.einsum("sd,sk->dk", rows, grad_pre, preferred_element_type=jnp.float32)
+    grad_weight_out = jnp.einsum(
+        "sh,sd->hd", gated_hidden, cotangent, preferred_element_type=jnp.float32
+    )
+    return mixed, grad_rows, gate_grad, grad_weight_in, grad_weight_out
+
+
+def bf16_pieces(x, count):
+    pieces = []
+    for _ in range(count):
+        piece = x.astype(jnp.bfloat16)
+        pieces.append(piece)
+        x = x - piece.astype(jnp.float32)
+    return pieces
+
+
+def dense_plan(tokens, grad_out, expert_ids, gates, w_in, w_out):
+    width = tokens.shape[1]
+    groups = lax.axis_size("expert")
+    mine = lax.axis_index("expert")
+    experts = jnp.arange(groups, dtype=jnp.int32)
+    onehot = expert_ids[:, :, None] == experts
+    dense_gates = jnp.sum(jnp.where(onehot, gates[:, :, None], 0.0), axis=1)
+    pieces = bf16_pieces(dense_gates, 3)
+    tail = jnp.zeros((tokens.shape[0], 128 - 3 * groups), jnp.bfloat16)
+    packed = jnp.concatenate([tokens, grad_out] + pieces + [tail], axis=1)
+    everyone = lax.all_gather(packed, ("dp", "expert"), axis=0, tiled=True)
+    rows = everyone[:, :width]
+    cotangent = everyone[:, width : 2 * width]
+    three = everyone[:, 2 * width : 2 * width + 3 * groups].astype(jnp.float32)
+    all_gates = three[:, :groups] + three[:, groups : 2 * groups] + three[:, 2 * groups :]
+    gate = jnp.sum(jnp.where(experts == mine, all_gates, 0.0), axis=1, keepdims=True)
+    half = w_out.shape[1]
+    mixed, grad_rows, gate_grad, grad_weight_in, grad_weight_out = expert_math(
+        rows, cotangent, gate, w_in.reshape(width, 2 * half), w_out[0]
+    )
+    spread = jnp.where(experts == mine, gate_grad, 0.0)
+    tail = jnp.zeros((rows.shape[0], 128 - 2 * groups), jnp.bfloat16)
+    partial = jnp.concatenate(
+        [mixed.astype(jnp.bfloat16), grad_rows.astype(jnp.bfloat16)]
+        + bf16_pieces(spread, 2)
+        + [tail],
+        axis=1,
+    )
+    total = lax.psum_scatter(partial, ("dp", "expert"), scatter_dimension=0, tiled=True)
+    two = total[:, 2 * width : 2 * width + 2 * groups].astype(jnp.float32)
+    by_expert = two[:, :groups] + two[:, groups:]
+    grad_gates = jnp.sum(jnp.where(onehot, by_expert[:, None, :], 0.0), axis=2)
+    return (
+        total[:, :width],
+        total[:, width : 2 * width],
+        grad_gates,
+        grad_weight_in.reshape(w_in.shape),
+        grad_weight_out[None],
+    )
+
+
+def per_device(tokens, grad_out, expert_ids, gates, w_in, w_out):
+    if lax.axis_size("expert") > 4 * expert_ids.shape[1]:
+        return routed_plan(tokens, grad_out, expert_ids, gates, w_in, w_out)
+    return dense_plan(tokens, grad_out, expert_ids, gates, w_in, w_out)
+
+
 def solution(mesh):
     in_specs = (
         P(("dp", "expert"), None),

time: 151 us -> 238 us (1.58)
  waiting for transfers between devices: 65.8 us -> 192 us
  starting transfers between devices: 24.1 us -> 0.08 us
  local copies, waits for them, and re-layouts: 25.8 us -> 15 us
  other arithmetic: 7.6 us -> 2.49 us
    unnamed x4 -> x3, waiting for transfers between devices: 1.41 us -> 129 us
    all_to_all x4 -> x0, waiting for transfers between devices: 62.3 us -> none  [the longest x1 17.5 us: per_device(): lax.all_to_all(grad_rows_in.reshape(groups, capacity, model_width), 'expe...]
    all_gather x2 -> x1, waiting for transfers between devices: 2.11 us -> 62.4 us  [dense_plan(): everyone = lax.all_gather(packed, ('dp', 'expert'), axis=0, tiled=True)]
    all_to_all x4 -> x0, starting transfers between devices: 23.9 us -> none  [the longest x1 7.39 us: per_device(): lax.all_to_all(send_rows, 'expert', split_axis=0, concat_axis=0, tiled=True)]
    gather x5 -> x0, local copies, waits for them, and re-layouts: 8.64 us -> none  [the longest x1 2.46 us: per_device(): slot_gate = gates_padded[inverse]]
    concatenate x2, local copies, waits for them, and re-layouts: 0.82 us -> 7.25 us  [the longest x1 5.69 us: dense_plan(): jnp.concatenate([mixed.astype(jnp.bfloat16), grad_rows.astype(jnp.bfloat1...]
    reshape x9 -> x0, local copies, waits for them, and re-layouts: 5 us -> none  [the longest x2 1.18 us: per_device(): rows = arrived_rows.reshape(groups * capacity, model_width)]
    unnamed x14 -> x13, local copies, waits for them, and re-layouts: 8.85 us -> 4.63 us
  transfers between devices with their start and end apart: 8 -> 2, of which waited for: 5 -> 2; matrix products, arithmetic and copies ran while one was open for 24% -> 4% of each run, Pallas kernels for 0% -> 0%
where the time goes in v1:
time: 238 us; the launch traced here: 237 us
  waiting for transfers between devices  192 us (81%)
  local copies, waits for them, and re-layouts  15 us (6%)
  between operations  14.2 us (6%)
  matrix products  13.8 us (6%)
  other arithmetic  2.49 us (1%)
    unnamed x3, waiting for transfers between devices  129 us
    all_gather x1, waiting for transfers between devices, dense_plan(): everyone = lax.all_gather(packed, ('dp', 'expert'), axis=0, tiled=True)  62.4 us
    concatenate x1, local copies, waits for them, and re-layouts, dense_plan(): jnp.concatenate([mixed.astype(jnp.bfloat16), grad_rows.astype(jnp.bfloat1...  5.69 us
  transfers between devices with their start and end apart: 2, of which 2 were waited for; matrix products, arithmetic and copies ran while one was open for 4% of the time, Pallas kernels for 0%

profile of v1, /device:TPU:0, one launch (start us, length us, event | category | flops | bytes accessed | tf_op | source)
XLA Modules:
  0.0 237.3 jit_solution(16125731765422691412)
XLA Ops:
  7.2 0.0 copy-start
  7.2 0.0 all-gather.2.cloned.1.call-start
  7.2 0.8 select_reduce_fusion.1
  8.0 0.1 copy.29
  8.1 0.1 copy.28
  8.2 0.1 copy.27
  8.3 1.6 concatenate.10
  9.8 0.0 all-gather.2.cloned.1.call-update
  9.9 0.0 all-reduce.3.cloned.1.call-start
  9.9 1.4 copy.36
  11.4 0.0 copy-start.1
  11.4 62.4 %all-gather.2.cloned.1.call-done = bf16[768,2176]{1,0:T(8,128)(2,1)} async-done(((bf16[24,2176]{1,0:T(8,128)(2,1)}), bf16[768,2176]{1,0:T(8,128)(2,1)}) %all-gather.2.cloned.1.call-update) | async-done | bytes 3342352 | tf_op jit(solution)/shard_map/all_gather | solution.py:160
  73.8 0.9 slice.52
  74.7 0.1 copy.35
  74.9 0.1 fusion.16
  74.9 2.5 %fusion.6 = f32[768,512]{0,1:T(8,128)S(1)} fusion(bf16[1024,512]{1,0:T(8,128)(2,1)S(1)} %bitcast.19, bf16[768,2176]{1,0:T(8,128)(2,1)} %all-gather.2.cloned.1.call-done), kind=kOutput, calls=%fused_computation.8 | convolution fusion | flops 805306368 | bytes 4194304 | tf_op jit(solution)/shard_map/dot_general | solution.py:119
  77.4 0.0 copy-done.1
  77.4 0.0 copy-done
  77.4 3.1 %multiply_convert_fusion.1 = (bf16[768,256]{0,1:T(8,128)(2,1)S(1)}, bf16[768,256]{0,1:T(8,128)(2,1)}, f32[768]{0:T(1024)S(1)}, bf16[768,256]{0,1:T(8,128)(2,1)S(1)}) fusion(f32[768,512]{0,1:T(8,128)S(1)} %fusion.6, f32[768]{0:T(1024)S(1)} %fusion.16, bf16[1,256,1024]{2,1,0:T(8,128)(2,1)S(1)} %copy-done, bf16[768,2176]{1,0:T(8,128)(2,1)} %all-gather.2.cloned.1.call-done), kind=kOutput, calls=%fused_computation.14 | convolution fusion | flops 406387968 | bytes 4855808 | tf_op jit(solution)/shard_map/sd,hd->sh/dot_general | solution.py:125
  80.5 0.1 fusion.14
  80.6 0.1 select_convert_fusion
  80.7 0.2 copy.31
  80.8 0.2 copy.32
  81.0 0.0 copy-start.2
  81.0 0.0 copy-start.4
  81.0 0.6 convolution_convert_fusion.1
  81.6 0.6 copy-done.2
  82.2 0.1 copy-done.4
  82.3 2.2 convolution_convert_fusion
  84.5 5.7 %concatenate.12 = bf16[768,2176]{1,0:T(8,128)(2,1)} concatenate(bf16[768,1024]{1,0:T(8,128)(2,1)S(1)} %convolution_convert_fusion.1, bf16[768,1024]{1,0:T(8,128)(2,1)} %convolution_convert_fusion, bf16[768,16]{1,0:T(8,128)(2,1)S(1)} %copy.31, bf16[768,16]{1,0:T(8,128)(2,1)S(1)} %copy.32, bf16[768,96]{1,0:T(8,128)(2,1)S(1)} %broadcast_in_dim.63), dimensions={1} | concatenate | bytes 6684672 | tf_op jit(solution)/shard_map/concatenate | solution.py:172
  90.2 0.0 all-reduce.3.cloned.1.call-update
  90.2 2.5 %fusion.4 = f32[1024,512]{0,1:T(8,128)S(1)} fusion(bf16[768,2176]{1,0:T(8,128)(2,1)} %all-gather.2.cloned.1.call-done, bf16[768,256]{0,1:T(8,128)(2,1)} %get-tuple-element.33, bf16[768,256]{0,1:T(8,128)(2,1)S(1)} %get-tuple-element.32), kind=kOutput, calls=%fused_computation.6 | convolution fusion | flops 806879232 | bytes 4456448 | tf_op jit(solution)/shard_map/sd,sk->dk/dot_general | solution.py:134
  92.8 2.3 copy.34
  95.1 0.0 copy-start.3
  95.1 3.0 %fusion.8 = f32[1,256,1024]{2,1,0:T(8,128)} fusion(bf16[768,256]{0,1:T(8,128)(2,1)S(1)} %get-tuple-element.35, bf16[768,2176]{1,0:T(8,128)(2,1)} %all-gather.2.cloned.1.call-done), kind=kOutput, calls=%fused_computation.10 | convolution fusion | flops 402653184 | bytes 3014656 | tf_op jit(solution)/shard_map/sh,sd->hd/dot_general | solution.py:135
  98.1 129.3 %all-reduce.3.cloned.1.call-done = bf16[768,2176]{1,0:T(8,128)(2,1)} async-done(((bf16[768,2176]{1,0:T(8,128)(2,1)}), bf16[768,2176]{1,0:T(8,128)(2,1)}) %all-reduce.3.cloned.1.call-update) | async-done | bytes 3342352
  227.4 0.8 dynamic-slice_convert_fusion
  228.2 0.1 slice_add_fusion.2
  228.3 0.1 copy.33
  228.3 0.0 copy-done.3
  228.3 0.6 select_reduce_fusion
  229.0 1.5 fusion.20
  (5 shorter events, 0.1 us)
Async XLA Ops:
  7.2 70.3 %copy-start = (bf16[1,256,1024]{2,1,0:T(8,128)(2,1)S(1)}, bf16[1,256,1024]{2,1,0:T(8,128)(2,1)}, u32[]{:S(2)}) copy-start(bf16[1,256,1024]{2,1,0:T(8,128)(2,1)} %param.11) | copy-start | bytes 1572868
  7.2 66.6 %all-gather.2.cloned.1.call-start = ((), (), s32[]{:S(2)}) async-start(), calls=%async_computation | async-start | bytes 3446784 | tf_op jit(solution)/shard_map/all_gather | solution.py:160
  9.9 217.6 %all-reduce.3.cloned.1.call-start = ((), (), s32[]{:S(2)}) async-start(), calls=%async_computation.1 | async-start | bytes 6684672
  11.4 66.1 %copy-start.1 = (bf16[128,8,2,256]{3,1,2,0:T(8,128)(2,1)}, bf16[128,8,2,256]{3,1,2,0:T(8,128)(2,1)S(1)}, u32[]{:S(2)}) copy-start(bf16[128,8,2,256]{3,1,2,0:T(8,128)(2,1)S(1)} %copy.36) | copy-start | bytes 3145732
  81.0 1.2 copy-start.2
  81.0 1.3 copy-start.4
  95.1 133.2 %copy-start.3 = (s32[24,8]{0,1:T(8,128)S(1)}, s32[24,8]{0,1:T(8,128)}, u32[]{:S(2)}) copy-start(s32[24,8]{0,1:T(8,128)} %param.8) | copy-start | bytes 2308
Sparse Core Ops, SparseCore 0:
  11.4 62.2 all-gather.1
  90.4 137.0 all-reduce.2

commit v2 on v0

--- a/solution.py
+++ b/solution.py
@@ -1,6 +1,10 @@
+import functools
+
 import jax
 import jax.numpy as jnp
 from jax import lax
+from jax.experimental import pallas as pl
+from jax.experimental.pallas import tpu as pltpu
 from jax.sharding import PartitionSpec as P
 
 
@@ -37,7 +41,7 @@
     return (grad_rows_in, grad_weight_in, grad_weight_out)
 
 
-def per_device(tokens, grad_out, expert_ids, gates, w_in, w_out):
+def routed_plan(tokens, grad_out, expert_ids, gates, w_in, w_out):
     count_tok, model_width = tokens.shape
     per_token = expert_ids.shape[1]
     groups = lax.axis_size("expert")
@@ -114,6 +118,315 @@
     return (mixed, grad_tokens, grad_gates, grad_in_shard, grad_out_shard)
 
 
+MESH = pl.DeviceIdType.MESH
+GATE_COLS = 128
+
+
+def dot_nt(a, b):
+    return lax.dot_general(a, b, (((1,), (1,)), ((), ())), preferred_element_type=jnp.float32)
+
+
+def dot_tn(a, b):
+    return lax.dot_general(a, b, (((0,), (0,)), ((), ())), preferred_element_type=jnp.float32)
+
+
+def moe_kernel(
+    groups, tokens_ref, cot_ref, ids_ref, gates_ref, w_in_ref, w_out_ref,
+    mixed_ref, grad_tok_ref, grad_gates_ref, grad_in_ref, grad_out_ref,
+    tok_all, cot_all, part_mixed, part_grad, recv_mixed, recv_grad,
+    rows_buf, cot_buf, hidden_buf, pre_buf,
+    gather_send, gather_recv, scatter_send, scatter_recv,
+):
+    count, width = tokens_ref.shape
+    per_token = ids_ref.shape[1]
+    half = w_out_ref.shape[0]
+    chunk = 8 * count
+    x = lax.axis_index("dp")
+    e = lax.axis_index("expert")
+    z, y, c = e // 4, (e // 2) % 2, e % 2
+
+    def place(px, pz, py, pc):
+        return (px, pz * 4 + py * 2 + pc)
+
+    to_z = {
+        1: place(x, z + 1 - 2 * (z % 2), y, c),
+        2: place(x, (z + 2) % 4, y, c),
+        3: place(x, 3 - z, y, c),
+    }
+    to_x = place(1 - x, z, y, c)
+    to_y = place(x, z, 1 - y, c)
+    to_core = place(x, z, y, 1 - c)
+
+    partners = [to_z[1], to_z[2], to_z[3], to_x, to_y, to_core]
+    barrier = pltpu.get_barrier_semaphore()
+    for partner in partners:
+        pl.semaphore_signal(barrier, inc=1, device_id=partner, device_id_type=MESH)
+
+    col = lax.broadcasted_iota(jnp.int32, (count, GATE_COLS), 1)
+    ids = ids_ref[...]
+    gates = gates_ref[...]
+    dense = jnp.zeros((count, GATE_COLS), jnp.float32)
+    for k in range(per_token):
+        dense = dense + jnp.where(ids[:, k : k + 1] == col % groups, gates[:, k : k + 1], 0.0)
+    high = dense.astype(jnp.bfloat16).astype(jnp.float32)
+    middle = (dense - high).astype(jnp.bfloat16).astype(jnp.float32)
+    low = dense - high - middle
+    pieces = jnp.where(
+        col < groups,
+        high,
+        jnp.where(col < 2 * groups, middle, jnp.where(col < 3 * groups, low, 0.0)),
+    )
+    tok_all[0, :, :width] = tokens_ref[...]
+    tok_all[0, :, width:] = pieces.astype(jnp.bfloat16)
+    cot_all[0] = cot_ref[...]
+    pl.semaphore_wait(barrier, len(partners))
+
+    gathered = (tok_all, cot_all)
+    sent = []
+
+    def push(h, src, dst, device):
+        copy = pltpu.make_async_remote_copy(
+            src_ref=gathered[h].at[src],
+            dst_ref=gathered[h].at[dst],
+            send_sem=gather_send.at[h, dst],
+            recv_sem=gather_recv.at[h, dst],
+            device_id=device,
+            device_id_type=MESH,
+        )
+        copy.start()
+        sent.append(copy)
+
+    def arrived(h, slot):
+        pltpu.make_async_remote_copy(
+            src_ref=gathered[h].at[slot],
+            dst_ref=gathered[h].at[slot],
+            send_sem=gather_send.at[h, slot],
+            recv_sem=gather_recv.at[h, slot],
+            device_id=to_core,
+            device_id_type=MESH,
+        ).wait_recv()
+
+    first = (to_x, to_y)
+    second = (to_y, to_x)
+    first_q = (2, 1)
+    second_q = (1, 2)
+    order = (0, 1, 3, 2)
+    for dz in (1, 3, 2):
+        for h in (0, 1):
+            push(h, 0, dz, to_z[dz])
+    for dz in order:
+        for h in (0, 1):
+            if dz:
+                arrived(h, dz)
+            push(h, dz, 8 * first_q[h] + dz, first[h])
+            push(h, dz, 8 * second_q[h] + dz, second[h])
+            push(h, dz, 4 + dz, to_core)
+    for dz in order:
+        for h in (0, 1):
+            slot = 8 * first_q[h] + dz
+            arrived(h, slot)
+            push(h, slot, 24 + dz, second[h])
+            push(h, slot, slot + 4, to_core)
+
+    partial = (part_mixed, part_grad)
+    landing = (recv_mixed, recv_grad)
+
+    def give(h, src, dst, device, number=1):
+        copy = pltpu.make_async_remote_copy(
+            src_ref=partial[h].at[pl.ds(src, number)],
+            dst_ref=landing[h].at[pl.ds(dst, number)],
+            send_sem=scatter_send.at[h, dst],
+            recv_sem=scatter_recv.at[h, dst],
+            device_id=device,
+            device_id_type=MESH,
+        )
+        copy.start()
+        sent.append(copy)
+
+    def took(h, dst, number=1):
+        pltpu.make_async_remote_copy(
+            src_ref=partial[h].at[pl.ds(0, number)],
+            dst_ref=landing[h].at[pl.ds(dst, number)],
+            send_sem=scatter_send.at[h, dst],
+            recv_sem=scatter_recv.at[h, dst],
+            device_id=to_core,
+            device_id_type=MESH,
+        ).wait_recv()
+
+    def add(h, slot, dst):
+        partial[h][slot] = (
+            partial[h][slot].astype(jnp.float32) + landing[h][dst].astype(jnp.float32)
+        ).astype(jnp.bfloat16)
+
+    wide_col = lax.broadcasted_iota(jnp.int32, (chunk, GATE_COLS), 1)
+
+    def compute(q):
+        block = pl.ds(8 * q, 8)
+        here = pl.ds(chunk * q, chunk)
+        packed = tok_all[block].astype(jnp.float32).reshape(chunk, width + GATE_COLS)
+        rows = packed[:, :width].astype(jnp.bfloat16)
+        cot = cot_all[block].astype(jnp.float32).reshape(chunk, width).astype(jnp.bfloat16)
+        own = jnp.logical_and(wide_col % groups == e, wide_col < 3 * groups)
+        gate = jnp.sum(jnp.where(own, packed[:, width:], 0.0), axis=1, keepdims=True)
+        rows_buf[here, :] = rows
+        cot_buf[here, :] = cot
+        preact = jnp.dot(rows, w_in_ref[...], preferred_element_type=jnp.float32)
+        gate_part = preact[:, :half]
+        up_part = preact[:, half:]
+        sig = jax.nn.sigmoid(gate_part)
+        activated = gate_part * sig
+        hidden = activated * up_part
+        back = dot_nt(cot, w_out_ref[...])
+        gate_grad = jnp.sum(hidden * back, axis=1, keepdims=True)
+        gated_hidden = (gate * hidden).astype(jnp.bfloat16)
+        gated_back = gate * back
+        grad_gate = gated_back * up_part * (sig * (1.0 + gate_part * (1.0 - sig)))
+        grad_up = gated_back * activated
+        grad_pre = jnp.concatenate([grad_gate, grad_up], axis=1).astype(jnp.bfloat16)
+        hidden_buf[here, :] = gated_hidden
+        pre_buf[here, :] = grad_pre
+        mixed = jnp.dot(gated_hidden, w_out_ref[...], preferred_element_type=jnp.float32)
+        part_mixed[block, :, :width] = mixed.reshape(8, count, width).astype(jnp.bfloat16)
+        high = gate_grad.astype(jnp.bfloat16).astype(jnp.float32)
+        spread = jnp.where(
+            wide_col == e, high, jnp.where(wide_col == groups + e, gate_grad - high, 0.0)
+        )
+        part_mixed[block, :, width:] = spread.reshape(8, count, GATE_COLS).astype(jnp.bfloat16)
+        grad_rows = dot_nt(grad_pre, w_in_ref[...])
+        part_grad[block] = grad_rows.reshape(8, count, width).astype(jnp.bfloat16)
+        for h in (0, 1):
+            give(h, 8 * q + 4, 4 * q, to_core, 4)
+
+    def fold_core(q):
+        for h in (0, 1):
+            took(h, 4 * q, 4)
+            for dz in range(4):
+                add(h, 8 * q + dz, 4 * q + dz)
+
+    def wait_core(q):
+        for dz in order:
+            for h in (0, 1):
+                arrived(h, 8 * q + 4 + dz)
+
+    wait_core(0)
+    compute(0)
+    for dz in order:
+        for h in (0, 1):
+            slot = 8 * second_q[h] + dz
+            arrived(h, slot)
+            push(h, slot, slot + 4, to_core)
+    wait_core(2)
+    compute(2)
+    wait_core(1)
+    compute(1)
+    for dz in order:
+        for h in (0, 1):
+            arrived(h, 24 + dz)
+            push(h, 24 + dz, 28 + dz, to_core)
+    fold_core(0)
+    one = (to_y, to_x)
+    two = (to_x, to_y)
+    back_order = (2, 3, 1, 0)
+    fold_core(2)
+    fold_core(1)
+    wait_core(3)
+    compute(3)
+    fold_core(3)
+    for dz in back_order:
+        for h in (0, 1):
+            give(h, 24 + dz, 20 + dz, one[h])
+    for dz in back_order:
+        for h in (0, 1):
+            give(h, 8 * (1, 2)[h] + dz, 16 + dz, one[h])
+    grad_out_ref[...] = dot_tn(hidden_buf[...], cot_buf[...])
+    for dz in back_order:
+        for h in (0, 1):
+            took(h, 20 + dz)
+            slot = 8 * (2, 1)[h] + dz
+            add(h, slot, 20 + dz)
+            give(h, slot, 24 + dz, two[h])
+    grad_in_ref[...] = dot_tn(rows_buf[...], pre_buf[...])
+    for dz in back_order:
+        for h in (0, 1):
+            took(h, 16 + dz)
+            add(h, dz, 16 + dz)
+            took(h, 24 + dz)
+            add(h, dz, 24 + dz)
+            if dz:
+                give(h, dz, 28 + dz, to_z[dz])
+    totals = []
+    for h in (0, 1):
+        total = partial[h][0].astype(jnp.float32)
+        for dz in (1, 3, 2):
+            took(h, 28 + dz)
+            total = total + landing[h][28 + dz].astype(jnp.float32)
+        totals.append(total)
+    mixed_ref[...] = totals[0][:, :width].astype(jnp.bfloat16)
+    grad_tok_ref[...] = totals[1].astype(jnp.bfloat16)
+    by_expert = totals[0][:, width:]
+    columns = []
+    for k in range(per_token):
+        chosen = jnp.logical_and(col % groups == ids[:, k : k + 1], col < 2 * groups)
+        columns.append(jnp.sum(jnp.where(chosen, by_expert, 0.0), axis=1, keepdims=True))
+    grad_gates_ref[...] = jnp.concatenate(columns, axis=1)
+    for copy in sent:
+        copy.wait_send()
+
+
+def dense_plan(tokens, grad_out, expert_ids, gates, w_in, w_out):
+    count, width = tokens.shape
+    groups = lax.axis_size("expert")
+    half = w_out.shape[1]
+    devices = 2 * groups
+    vmem = pl.BlockSpec(memory_space=pltpu.VMEM)
+    total_rows = devices * count
+    wide = width + GATE_COLS
+    outs = pl.pallas_call(
+        functools.partial(moe_kernel, groups),
+        out_shape=(
+            jax.ShapeDtypeStruct((count, width), jnp.bfloat16),
+            jax.ShapeDtypeStruct((count, width), jnp.bfloat16),
+            jax.ShapeDtypeStruct(gates.shape, jnp.float32),
+            jax.ShapeDtypeStruct((width, 2 * half), jnp.float32),
+            jax.ShapeDtypeStruct((half, width), jnp.float32),
+        ),
+        in_specs=[vmem] * 6,
+        out_specs=[vmem] * 5,
+        scratch_shapes=[
+            pltpu.VMEM((devices, count, wide), jnp.bfloat16),
+            pltpu.VMEM((devices, count, width), jnp.bfloat16),
+            pltpu.VMEM((devices, count, wide), jnp.bfloat16),
+            pltpu.VMEM((devices, count, width), jnp.bfloat16),
+            pltpu.VMEM((devices, count, wide), jnp.bfloat16),
+            pltpu.VMEM((devices, count, width), jnp.bfloat16),
+            pltpu.VMEM((total_rows, width), jnp.bfloat16),
+            pltpu.VMEM((total_rows, width), jnp.bfloat16),
+            pltpu.VMEM((total_rows, half), jnp.bfloat16),
+            pltpu.VMEM((total_rows, 2 * half), jnp.bfloat16),
+            pltpu.SemaphoreType.DMA((2, devices)),
+            pltpu.SemaphoreType.DMA((2, devices)),
+            pltpu.SemaphoreType.DMA((2, devices)),
+            pltpu.SemaphoreType.DMA((2, devices)),
+        ],
+        compiler_params=pltpu.CompilerParams(
+            collective_id=0, has_side_effects=True, vmem_limit_bytes=52 * 1024 * 1024
+        ),
+        cost_estimate=pl.CostEstimate(
+            flops=18 * total_rows * width * half,
+            bytes_accessed=12 * width * half + 6 * width * half,
+            transcendentals=total_rows * half,
+        ),
+    )(tokens, grad_out, expert_ids, gates, w_in.reshape(width, 2 * half), w_out[0])
+    mixed, grad_tokens, grad_gates, grad_in, grad_out_w = outs
+    return (mixed, grad_tokens, grad_gates, grad_in.reshape(w_in.shape), grad_out_w[None])
+
+
+def per_device(tokens, grad_out, expert_ids, gates, w_in, w_out):
+    if lax.axis_size("expert") == 16 and lax.axis_size("dp") == 2:
+        return dense_plan(tokens, grad_out, expert_ids, gates, w_in, w_out)
+    return routed_plan(tokens, grad_out, expert_ids, gates, w_in, w_out)
+
+
 def solution(mesh):
     in_specs = (
         P(("dp", "expert"), None),

time: 151 us -> 66.3 us (0.44)
  the two profiles are of different devices: /device:TPU:0 before, /device:TPU:1 now
where the time goes in v2:
time: 66.3 us; the launch traced here: 66.1 us
  Pallas kernels  55 us (83%)
  local copies, waits for them, and re-layouts  10.4 us (16%)
  between operations  0.67 us (1%)
    pallas_call x1, Pallas kernels, dense_plan(): pl.pallas_call(functools.partial(moe_kernel, groups), out_shape=(jax.Shap...  55 us
    unnamed x13, local copies, waits for them, and re-layouts  6.87 us
    reshape x1, local copies, waits for them, and re-layouts, dense_plan(): grad_in.reshape(w_in.shape)  3.51 us

profile of v2, /device:TPU:1, one launch (start us, length us, event | category | flops | bytes accessed | tf_op | source)
XLA Modules:
  0.0 66.1 jit_solution(14724433745656937939)
XLA Ops:
  0.6 0.0 copy-start
  0.6 0.0 copy-start.2
  0.7 0.0 copy-start.1
  0.7 0.8 %copy.11.ids_ref = s32[24,8]{1,0:T(8,128)S(1)} copy(s32[24,8]{0,1:T(8,128)} %param.8) | data formatting | bytes 1536 | tf_op args[2]
  1.5 0.8 %copy.12.gates_ref = f32[24,8]{1,0:T(8,128)S(1)} copy(f32[24,8]{0,1:T(8,128)} %param.9) | data formatting | bytes 1536 | tf_op args[3]
  2.2 2.4 %copy.14 = bf16[128,8,2,256]{3,1,2,0:T(8,128)(2,1)} copy(bf16[128,8,2,256]{3,2,1,0:T(2,128)(2,1)} %bitcast.7) | data formatting | bytes 2097152
  4.7 0.0 copy-done
  4.7 0.0 copy-done.2
  4.7 0.0 copy-done.1
  4.7 55.0 %shard_map.101 = (bf16[24,1024]{1,0:T(8,128)(2,1)S(1)}, bf16[24,1024]{1,0:T(8,128)(2,1)S(1)}, f32[24,8]{1,0:T(8,128)S(1)}, f32[1024,512]{1,0:T(8,128)}, f32[256,1024]{1,0:T(8,128)S(1)}) custom-call(bf16[24,1024]{1,0:T(8,128)(2,1)S(1)} %copy-done.1, bf16[24,1024]{1,0:T(8,128)(2,1)S(1)} %copy-done.2, s32[24,8]{1,0:T(8,128)S(1)} %copy.11.ids_ref, ...), custom_call_target="tpu_custom_call" | custom-call | flops 3623878656 | bytes 4718592 | tf_op jit(solution)/shard_map/pallas_call | solution.py:384
  59.7 0.7 %copy.13 = f32[24,8]{0,1:T(8,128)} copy(f32[24,8]{1,0:T(8,128)S(1)} %get-tuple-element.17) | data formatting | bytes 1536
  60.4 3.5 %reshape.17 = f32[1,1024,2,256]{3,2,1,0:T(2,128)} reshape(f32[1024,512]{1,0:T(8,128)} %get-tuple-element.13) | data formatting | bytes 4194304 | tf_op jit(solution)/shard_map/reshape | solution.py:421
  63.9 0.6 copy.18
  64.5 0.6 copy.19
  65.1 1.0 %copy.20 = f32[1,256,1024]{2,1,0:T(8,128)} copy(f32[1,256,1024]{2,1,0:T(8,128)S(1)} %bitcast.5) | data formatting | bytes 2097152
Async XLA Ops:
  0.6 4.0 %copy-start = (bf16[1,256,1024]{2,1,0:T(8,128)(2,1)S(1)}, bf16[1,256,1024]{2,1,0:T(8,128)(2,1)}, u32[]{:S(2)}) copy-start(bf16[1,256,1024]{2,1,0:T(8,128)(2,1)} %param.11) | copy-start | bytes 1572868
  0.6 4.0 %copy-start.2 = (bf16[24,1024]{1,0:T(8,128)(2,1)S(1)}, bf16[24,1024]{1,0:T(8,128)(2,1)}, u32[]{:S(2)}) copy-start(bf16[24,1024]{1,0:T(8,128)(2,1)} %cot_ref.1) | copy-start | bytes 147460
  0.7 4.0 %copy-start.1 = (bf16[24,1024]{1,0:T(8,128)(2,1)S(1)}, bf16[24,1024]{1,0:T(8,128)(2,1)}, u32[]{:S(2)}) copy-start(bf16[24,1024]{1,0:T(8,128)(2,1)} %tokens_ref.1) | copy-start | bytes 147460

commit v3 on v0

--- a/solution.py
+++ b/solution.py
@@ -1,6 +1,10 @@
+import functools
+
 import jax
 import jax.numpy as jnp
 from jax import lax
+from jax.experimental import pallas as pl
+from jax.experimental.pallas import tpu as pltpu
 from jax.sharding import PartitionSpec as P
 
 
@@ -37,7 +41,7 @@
     return (grad_rows_in, grad_weight_in, grad_weight_out)
 
 
-def per_device(tokens, grad_out, expert_ids, gates, w_in, w_out):
+def routed_plan(tokens, grad_out, expert_ids, gates, w_in, w_out):
     count_tok, model_width = tokens.shape
     per_token = expert_ids.shape[1]
     groups = lax.axis_size("expert")
@@ -114,6 +118,368 @@
     return (mixed, grad_tokens, grad_gates, grad_in_shard, grad_out_shard)
 
 
+MESH = pl.DeviceIdType.MESH
+GATE_COLS = 128
+
+
+def dot_nt(a, b):
+    return lax.dot_general(a, b, (((1,), (1,)), ((), ())), preferred_element_type=jnp.float32)
+
+
+def dot_tn(a, b):
+    return lax.dot_general(a, b, (((0,), (0,)), ((), ())), preferred_element_type=jnp.float32)
+
+
+def moe_kernel(
+    groups, tokens_ref, cot_ref, ids_ref, gates_ref, w_in_hbm, w_out_hbm,
+    mixed_ref, grad_tok_ref, grad_gates_ref, grad_in_hbm, grad_out_hbm,
+    tok_all, cot_all, part_mixed, part_grad, recv_mixed, recv_grad,
+    rows_buf, cot_buf, hidden_buf, pre_buf, w_in_ref, w_out_ref, grad_in_ref, grad_out_ref,
+    gather_send, gather_recv, scatter_send, scatter_recv, local_sem,
+):
+    count, width = tokens_ref.shape
+    per_token = ids_ref.shape[0]
+    half = w_out_ref.shape[0]
+    batches, blocks, batch = tok_all.shape[:3]
+    chunk = blocks * batch
+    x = lax.axis_index("dp")
+    e = lax.axis_index("expert")
+    z, y, c = e // 4, (e // 2) % 2, e % 2
+
+    def place(px, pz, py, pc):
+        return (px, pz * 4 + py * 2 + pc)
+
+    to_z = {
+        1: place(x, z + 1 - 2 * (z % 2), y, c),
+        2: place(x, (z + 2) % 4, y, c),
+        3: place(x, 3 - z, y, c),
+    }
+    to_x = place(1 - x, z, y, c)
+    to_y = place(x, z, 1 - y, c)
+    to_core = place(x, z, y, 1 - c)
+
+    partners = [to_z[1], to_z[2], to_z[3], to_x, to_y, to_core]
+    barrier = pltpu.get_barrier_semaphore()
+    for partner in partners:
+        pl.semaphore_signal(barrier, inc=1, device_id=partner, device_id_type=MESH)
+    load_in = pltpu.make_async_copy(w_in_hbm, w_in_ref, local_sem.at[0])
+    load_out = pltpu.make_async_copy(w_out_hbm, w_out_ref, local_sem.at[1])
+    load_in.start()
+    load_out.start()
+
+    col = lax.broadcasted_iota(jnp.int32, (count, GATE_COLS), 1)
+    col_expert = (col % groups).astype(jnp.float32)
+    diagonal = lax.broadcasted_iota(jnp.int32, (count, count), 0) == lax.broadcasted_iota(
+        jnp.int32, (count, count), 1
+    )
+    ids_t = ids_ref[...].astype(jnp.float32)
+    gates_t = gates_ref[...]
+
+    def column(table, k):
+        return jnp.sum(jnp.where(diagonal, table[k : k + 1, :], 0.0), axis=1, keepdims=True)
+
+    ids = [column(ids_t, k) for k in range(per_token)]
+    dense = jnp.zeros((count, GATE_COLS), jnp.float32)
+    for k in range(per_token):
+        dense = dense + jnp.where(ids[k] == col_expert, column(gates_t, k), 0.0)
+    high = dense.astype(jnp.bfloat16).astype(jnp.float32)
+    middle = (dense - high).astype(jnp.bfloat16).astype(jnp.float32)
+    low = dense - high - middle
+    pieces = jnp.where(
+        col < groups,
+        high,
+        jnp.where(col < 2 * groups, middle, jnp.where(col < 3 * groups, low, 0.0)),
+    )
+    own_tokens = tokens_ref[...].astype(jnp.float32)
+    own_cot = cot_ref[...].astype(jnp.float32)
+    for g in range(batches):
+        part = slice(g * batch, (g + 1) * batch)
+        tok_all[g, 0, :, :width] = own_tokens[part].astype(jnp.bfloat16)
+        tok_all[g, 0, :, width:] = pieces[part].astype(jnp.bfloat16)
+        cot_all[g, 0] = own_cot[part].astype(jnp.bfloat16)
+    pl.semaphore_wait(barrier, len(partners))
+
+    gathered = (tok_all, cot_all)
+    partial = (part_mixed, part_grad)
+    landing = (recv_mixed, recv_grad)
+    sent = []
+
+    def copy_of(source, target, sems, g, h, src, dst, device, number):
+        return pltpu.make_async_remote_copy(
+            src_ref=source[h].at[g, pl.ds(src, number)],
+            dst_ref=target[h].at[g, pl.ds(dst, number)],
+            send_sem=sems[0].at[g, h, dst],
+            recv_sem=sems[1].at[g, h, dst],
+            device_id=device,
+            device_id_type=MESH,
+        )
+
+    gather_sems = (gather_send, gather_recv)
+    scatter_sems = (scatter_send, scatter_recv)
+
+    def push(g, h, src, dst, device, number=4):
+        copy = copy_of(gathered, gathered, gather_sems, g, h, src, dst, device, number)
+        copy.start()
+        sent.append(copy)
+
+    def arrived(g, h, slot, number=4):
+        copy_of(gathered, gathered, gather_sems, g, h, slot, slot, to_core, number).wait_recv()
+
+    def give(g, h, src, dst, device, number=4):
+        copy = copy_of(partial, landing, scatter_sems, g, h, src, dst, device, number)
+        copy.start()
+        sent.append(copy)
+
+    def took(g, h, dst, number=4):
+        copy_of(partial, landing, scatter_sems, g, h, 0, dst, to_core, number).wait_recv()
+
+    def add(g, h, slot, dst, number=4):
+        here = pl.ds(slot, number)
+        partial[h][g, here] = (
+            partial[h][g, here].astype(jnp.float32)
+            + landing[h][g, pl.ds(dst, number)].astype(jnp.float32)
+        ).astype(jnp.bfloat16)
+
+    first = (to_x, to_y)
+    second = (to_y, to_x)
+    first_slot = (8, 4)
+    second_slot = (4, 8)
+
+    def gather_z(g):
+        for dz in (1, 3, 2):
+            for h in (0, 1):
+                push(g, h, 0, dz, to_z[dz], 1)
+
+    def gather_plane(g):
+        for h in (0, 1):
+            for dz in (1, 3, 2):
+                arrived(g, h, dz, 1)
+            push(g, h, 0, first_slot[h], first[h])
+            push(g, h, 0, second_slot[h], second[h])
+            push(g, h, 0, 16, to_core)
+
+    def gather_far(g):
+        for h in (0, 1):
+            slot = first_slot[h]
+            arrived(g, h, slot)
+            push(g, h, slot, 12, second[h])
+            push(g, h, slot, 16 + slot, to_core)
+
+    def gather_core(g):
+        for h in (0, 1):
+            slot = second_slot[h]
+            arrived(g, h, slot)
+            push(g, h, slot, 16 + slot, to_core)
+        for h in (0, 1):
+            arrived(g, h, 12)
+            push(g, h, 12, 28, to_core)
+
+    def gather_end(g):
+        for slot in (16, 20, 24, 28):
+            for h in (0, 1):
+                arrived(g, h, slot)
+
+    wide_col = lax.broadcasted_iota(jnp.int32, (chunk, GATE_COLS), 1)
+
+    def compute(g):
+        here = pl.ds(chunk * g, chunk)
+        packed = tok_all[g].astype(jnp.float32).reshape(chunk, width + GATE_COLS)
+        rows = packed[:, :width].astype(jnp.bfloat16)
+        cot = cot_all[g].astype(jnp.float32).reshape(chunk, width).astype(jnp.bfloat16)
+        own = jnp.logical_and(wide_col % groups == e, wide_col < 3 * groups)
+        gate = jnp.sum(jnp.where(own, packed[:, width:], 0.0), axis=1, keepdims=True)
+        rows_buf[here, :] = rows
+        cot_buf[here, :] = cot
+        preact = jnp.dot(rows, w_in_ref[...], preferred_element_type=jnp.float32)
+        gate_part = preact[:, :half]
+        up_part = preact[:, half:]
+        sig = jax.nn.sigmoid(gate_part)
+        activated = gate_part * sig
+        hidden = activated * up_part
+        back = dot_nt(cot, w_out_ref[...])
+        gate_grad = jnp.sum(hidden * back, axis=1, keepdims=True)
+        gated_hidden = (gate * hidden).astype(jnp.bfloat16)
+        gated_back = gate * back
+        grad_gate = gated_back * up_part * (sig * (1.0 + gate_part * (1.0 - sig)))
+        grad_up = gated_back * activated
+        grad_pre = jnp.concatenate([grad_gate, grad_up], axis=1).astype(jnp.bfloat16)
+        hidden_buf[here, :] = gated_hidden
+        pre_buf[here, :] = grad_pre
+        mixed = jnp.dot(gated_hidden, w_out_ref[...], preferred_element_type=jnp.float32)
+        part_mixed[g, :, :, :width] = mixed.reshape(blocks, batch, width).astype(jnp.bfloat16)
+        high = gate_grad.astype(jnp.bfloat16).astype(jnp.float32)
+        spread = jnp.where(
+            wide_col == e, high, jnp.where(wide_col == groups + e, gate_grad - high, 0.0)
+        )
+        part_mixed[g, :, :, width:] = spread.reshape(blocks, batch, GATE_COLS).astype(
+            jnp.bfloat16
+        )
+        give(g, 0, 16, 0, to_core, 16)
+        grad_rows = dot_nt(grad_pre, w_in_ref[...])
+        part_grad[g] = grad_rows.reshape(blocks, batch, width).astype(jnp.bfloat16)
+        give(g, 1, 16, 0, to_core, 16)
+
+    def scatter_plane(g):
+        for h in (0, 1):
+            took(g, h, 0, 16)
+            add(g, h, 12, 12)
+            give(g, h, 12, 20, second[h])
+        for h in (0, 1):
+            add(g, h, second_slot[h], second_slot[h])
+            give(g, h, second_slot[h], 16, second[h])
+        for h in (0, 1):
+            add(g, h, first_slot[h], first_slot[h])
+            add(g, h, 0, 0)
+
+    def scatter_near(g):
+        for h in (0, 1):
+            took(g, h, 20)
+            add(g, h, first_slot[h], 20)
+            give(g, h, first_slot[h], 24, first[h])
+
+    def scatter_z(g):
+        for h in (0, 1):
+            took(g, h, 16)
+            add(g, h, 0, 16)
+        for h in (0, 1):
+            took(g, h, 24)
+            add(g, h, 0, 24)
+            for dz in (2, 3, 1):
+                give(g, h, dz, 28 + dz, to_z[dz], 1)
+
+    totals = ([], [])
+
+    def scatter_end(g):
+        for h in (0, 1):
+            total = partial[h][g, 0].astype(jnp.float32)
+            for dz in (1, 3, 2):
+                took(g, h, 28 + dz, 1)
+                total = total + landing[h][g, 28 + dz].astype(jnp.float32)
+            totals[h].append(total)
+
+    for g in range(batches):
+        gather_z(g)
+    gather_plane(0)
+    gather_plane(1)
+    gather_far(0)
+    gather_plane(2)
+    gather_core(0)
+    gather_far(1)
+    gather_end(0)
+    load_in.wait()
+    load_out.wait()
+    compute(0)
+    gather_core(1)
+    gather_far(2)
+    scatter_plane(0)
+    gather_end(1)
+    compute(1)
+    gather_core(2)
+    scatter_near(0)
+    scatter_plane(1)
+    gather_end(2)
+    compute(2)
+    scatter_z(0)
+    scatter_near(1)
+    scatter_plane(2)
+    grad_out_ref[...] = dot_tn(hidden_buf[...], cot_buf[...])
+    save_out = pltpu.make_async_copy(grad_out_ref, grad_out_hbm, local_sem.at[1])
+    save_out.start()
+    scatter_z(1)
+    scatter_near(2)
+    tiles = half // 128
+    grad_in = dot_tn(rows_buf[...], pre_buf[...])
+    for tile in range(tiles):
+        for side in range(2):
+            left = side * half + tile * 128
+            grad_in_ref[pl.ds(tile * 2 + side, width, stride=2 * tiles), :] = grad_in[
+                :, left : left + 128
+            ]
+    save_in = pltpu.make_async_copy(grad_in_ref, grad_in_hbm, local_sem.at[0])
+    save_in.start()
+    scatter_z(2)
+    for g in range(batches):
+        scatter_end(g)
+    total_mixed = jnp.concatenate(totals[0], axis=0)
+    mixed_ref[...] = total_mixed[:, :width].astype(jnp.bfloat16)
+    grad_tok_ref[...] = jnp.concatenate(totals[1], axis=0).astype(jnp.bfloat16)
+    by_expert = total_mixed[:, width:]
+    lines = []
+    for k in range(per_token):
+        chosen = jnp.logical_and(ids[k] == col_expert, col < 2 * groups)
+        value = jnp.sum(jnp.where(chosen, by_expert, 0.0), axis=1, keepdims=True)
+        lines.append(jnp.sum(jnp.where(diagonal, value, 0.0), axis=0, keepdims=True))
+    grad_gates_ref[...] = jnp.concatenate(lines, axis=0)
+    save_out.wait()
+    save_in.wait()
+    for copy in sent:
+        copy.wait_send()
+
+
+def dense_plan(tokens, grad_out, expert_ids, gates, w_in, w_out):
+    count, width = tokens.shape
+    groups = lax.axis_size("expert")
+    half = w_out.shape[1]
+    devices = 2 * groups
+    batch = 8
+    batches = count // batch
+    vmem = pl.BlockSpec(memory_space=pltpu.VMEM)
+    anywhere = pl.BlockSpec(memory_space=pl.ANY)
+    total_rows = devices * count
+    wide = width + GATE_COLS
+    tiles = half // 128
+    outs = pl.pallas_call(
+        functools.partial(moe_kernel, groups),
+        out_shape=(
+            jax.ShapeDtypeStruct((count, width), jnp.bfloat16),
+            jax.ShapeDtypeStruct((count, width), jnp.bfloat16),
+            jax.ShapeDtypeStruct(gates.shape[::-1], jnp.float32),
+            jax.ShapeDtypeStruct((width * 2 * tiles, 128), jnp.float32),
+            jax.ShapeDtypeStruct((half, width), jnp.float32),
+        ),
+        in_specs=[vmem] * 4 + [anywhere] * 2,
+        out_specs=[vmem] * 3 + [anywhere] * 2,
+        scratch_shapes=[
+            pltpu.VMEM((batches, devices, batch, wide), jnp.bfloat16),
+            pltpu.VMEM((batches, devices, batch, width), jnp.bfloat16),
+            pltpu.VMEM((batches, devices, batch, wide), jnp.bfloat16),
+            pltpu.VMEM((batches, devices, batch, width), jnp.bfloat16),
+            pltpu.VMEM((batches, devices, batch, wide), jnp.bfloat16),
+            pltpu.VMEM((batches, devices, batch, width), jnp.bfloat16),
+            pltpu.VMEM((total_rows, width), jnp.bfloat16),
+            pltpu.VMEM((total_rows, width), jnp.bfloat16),
+            pltpu.VMEM((total_rows, half), jnp.bfloat16),
+            pltpu.VMEM((total_rows, 2 * half), jnp.bfloat16),
+            pltpu.VMEM((width, 2 * half), jnp.bfloat16),
+            pltpu.VMEM((half, width), jnp.bfloat16),
+            pltpu.VMEM((width * 2 * tiles, 128), jnp.float32),
+            pltpu.VMEM((half, width), jnp.float32),
+            pltpu.SemaphoreType.DMA((batches, 2, devices)),
+            pltpu.SemaphoreType.DMA((batches, 2, devices)),
+            pltpu.SemaphoreType.DMA((batches, 2, devices)),
+            pltpu.SemaphoreType.DMA((batches, 2, devices)),
+            pltpu.SemaphoreType.DMA((2,)),
+        ],
+        compiler_params=pltpu.CompilerParams(
+            collective_id=0, has_side_effects=True, vmem_limit_bytes=44 * 1024 * 1024
+        ),
+        cost_estimate=pl.CostEstimate(
+            flops=18 * total_rows * width * half,
+            bytes_accessed=12 * width * half + 6 * width * half,
+            transcendentals=total_rows * half,
+        ),
+    )(tokens, grad_out, expert_ids.T, gates.T, w_in.reshape(width, 2 * half), w_out[0])
+    mixed, grad_tokens, grad_gates, grad_in, grad_out_w = outs
+    grad_in = grad_in.reshape(width, tiles, 2, 128).transpose(0, 2, 1, 3).reshape(w_in.shape)
+    return (mixed, grad_tokens, grad_gates.T, grad_in, grad_out_w[None])
+
+
+def per_device(tokens, grad_out, expert_ids, gates, w_in, w_out):
+    if lax.axis_size("expert") == 16 and lax.axis_size("dp") == 2:
+        return dense_plan(tokens, grad_out, expert_ids, gates, w_in, w_out)
+    return routed_plan(tokens, grad_out, expert_ids, gates, w_in, w_out)
+
+
 def solution(mesh):
     in_specs = (
         P(("dp", "expert"), None),

time: 151 us -> 60.6 us (0.40)
  waiting for transfers between devices: 65.8 us -> 0 us
  Pallas kernels: 0 us -> 54.1 us
  starting transfers between devices: 24.1 us -> 0 us
  local copies, waits for them, and re-layouts: 25.8 us -> 5.64 us
  between operations: 14 us -> 0.73 us
  matrix products: 13.1 us -> 0 us
  other arithmetic: 7.6 us -> 0 us
    all_to_all x4 -> x0, waiting for transfers between devices: 62.3 us -> none  [the longest x1 17.5 us: per_device(): lax.all_to_all(grad_rows_in.reshape(groups, capacity, model_width), 'expe...]
    pallas_call x0 -> x1, Pallas kernels: none -> 54.1 us  [dense_plan(): pl.pallas_call(functools.partial(moe_kernel, groups), out_shape=(jax.Shap...]
    all_to_all x4 -> x0, starting transfers between devices: 23.9 us -> none  [the longest x1 7.39 us: per_device(): lax.all_to_all(send_rows, 'expert', split_axis=0, concat_axis=0, tiled=True)]
    dot_general x7 -> x0, matrix products: 13.1 us -> none  [the longest x1 3.02 us: backward_part(): jnp.einsum('sd,hd->sh', grad_rows, weight_out, preferred_element_type=jnp...]
    gather x5 -> x0, local copies, waits for them, and re-layouts: 8.64 us -> none  [the longest x1 2.46 us: per_device(): slot_gate = gates_padded[inverse]]
    reshape x9 -> x0, local copies, waits for them, and re-layouts: 5 us -> none  [the longest x2 1.18 us: per_device(): rows = arrived_rows.reshape(groups * capacity, model_width)]
    unnamed x14 -> x16, local copies, waits for them, and re-layouts: 8.85 us -> 5.64 us
    convert_element_type x2 -> x0, other arithmetic: 3.16 us -> none  [the longest x1 2.13 us: per_device(): grad_in_shard, grad_out_shard = (lax.psum_scatter(grad_weight_in.reshape(...]
  transfers between devices with their start and end apart: 8 -> 0, of which waited for: 5 -> 0; matrix products, arithmetic and copies ran while one was open for 24% -> 0% of each run, Pallas kernels for 0% -> 0%
where the time goes in v3:
time: 60.6 us; the launch traced here: 60.4 us
  Pallas kernels  54.1 us (89%)
  local copies, waits for them, and re-layouts  5.64 us (9%)
  between operations  0.73 us (1%)
    pallas_call x1, Pallas kernels, dense_plan(): pl.pallas_call(functools.partial(moe_kernel, groups), out_shape=(jax.Shap...  54.1 us
    unnamed x16, local copies, waits for them, and re-layouts  5.64 us

profile of v3, /device:TPU:0, one launch (start us, length us, event | category | flops | bytes accessed | tf_op | source)
XLA Modules:
  0.0 60.4 jit_solution(14155407569809884061)
XLA Ops:
  0.6 0.0 copy-start
  0.6 0.0 copy-start.4
  0.7 0.0 copy-start.3
  0.7 0.0 copy-start.2
  0.7 0.0 copy-start.1
  0.7 1.5 %copy.12 = bf16[128,8,2,256]{3,1,2,0:T(8,128)(2,1)S(1)} copy(bf16[128,8,2,256]{3,2,1,0:T(2,128)(2,1)} %bitcast.20) | data formatting | bytes 2097152
  2.2 0.0 copy-done
  2.2 0.0 copy-done.4
  2.2 0.0 copy-done.3
  2.2 0.0 copy-done.2
  2.2 0.0 copy-done.1
  2.2 54.1 %shard_map.101 = (bf16[24,1024]{1,0:T(8,128)(2,1)S(1)}, bf16[24,1024]{1,0:T(8,128)(2,1)S(1)}, f32[8,24]{1,0:T(8,128)S(1)}, f32[4096,128]{1,0:T(8,128)S(1)}, f32[256,1024]{1,0:T(8,128)S(1)}) custom-call(bf16[24,1024]{1,0:T(8,128)(2,1)S(1)} %copy-done.1, bf16[24,1024]{1,0:T(8,128)(2,1)S(1)} %copy-done.2, s32[8,24]{1,0:T(8,128)S(1)} %bitcast.18, ...), custom_call_target="tpu_custom_call" | custom-call | flops 3623878656 | bytes 4718592 | tf_op jit(solution)/shard_map/pallas_call | solution.py:431
  56.3 0.6 %copy.18 = bf16[24,1024]{1,0:T(8,128)(2,1)} copy(bf16[24,1024]{1,0:T(8,128)(2,1)S(1)} %get-tuple-element.20) | data formatting | bytes 98304
  56.9 0.6 %copy.19 = bf16[24,1024]{1,0:T(8,128)(2,1)} copy(bf16[24,1024]{1,0:T(8,128)(2,1)S(1)} %get-tuple-element.21) | data formatting | bytes 98304
  57.6 0.6 copy.20
  58.2 1.3 %copy.21 = f32[1,1024,2,256]{3,2,1,0:T(2,128)} copy(f32[1,1024,2,256]{3,2,1,0:T(2,128)S(1)} %bitcast.13) | data formatting | bytes 4194304
  59.5 1.0 %copy.22 = f32[1,256,1024]{2,1,0:T(8,128)} copy(f32[1,256,1024]{2,1,0:T(8,128)S(1)} %bitcast.14) | data formatting | bytes 2097152
Async XLA Ops:
  0.6 1.6 %copy-start = (bf16[1,256,1024]{2,1,0:T(8,128)(2,1)S(1)}, bf16[1,256,1024]{2,1,0:T(8,128)(2,1)}, u32[]{:S(2)}) copy-start(bf16[1,256,1024]{2,1,0:T(8,128)(2,1)} %param.11) | copy-start | bytes 1572868
  0.6 1.6 %copy-start.4 = (f32[24,8]{0,1:T(8,128)S(1)}, f32[24,8]{0,1:T(8,128)}, u32[]{:S(2)}) copy-start(f32[24,8]{0,1:T(8,128)} %param.9) | copy-start | bytes 2308
  0.7 1.6 %copy-start.3 = (s32[24,8]{0,1:T(8,128)S(1)}, s32[24,8]{0,1:T(8,128)}, u32[]{:S(2)}) copy-start(s32[24,8]{0,1:T(8,128)} %param.8) | copy-start | bytes 2308
  0.7 1.6 %copy-start.2 = (bf16[24,1024]{1,0:T(8,128)(2,1)S(1)}, bf16[24,1024]{1,0:T(8,128)(2,1)}, u32[]{:S(2)}) copy-start(bf16[24,1024]{1,0:T(8,128)(2,1)} %cot_ref.1) | copy-start | bytes 147460
  0.7 1.6 %copy-start.1 = (bf16[24,1024]{1,0:T(8,128)(2,1)S(1)}, bf16[24,1024]{1,0:T(8,128)(2,1)}, u32[]{:S(2)}) copy-start(bf16[24,1024]{1,0:T(8,128)(2,1)} %tokens_ref.1) | copy-start | bytes 147460

commit v4 on v3

--- a/solution.py
+++ b/solution.py
@@ -245,30 +245,57 @@
     first_slot = (8, 4)
     second_slot = (4, 8)
 
+    plane_first = [g == 1 for g in range(batches)]
+
     def gather_z(g):
         for dz in (1, 3, 2):
             for h in (0, 1):
                 push(g, h, 0, dz, to_z[dz], 1)
 
+    def gather_own(g):
+        for h in (0, 1):
+            push(g, h, 0, first_slot[h], first[h], 1)
+        if not plane_first[g]:
+            for h in (0, 1):
+                push(g, h, 0, second_slot[h], second[h], 1)
+
     def gather_plane(g):
+        if plane_first[g]:
+            for h in (0, 1):
+                slot = first_slot[h]
+                arrived(g, h, slot, 1)
+                for dz in (1, 3, 2):
+                    push(g, h, slot, slot + dz, to_z[dz], 1)
         for h in (0, 1):
             for dz in (1, 3, 2):
                 arrived(g, h, dz, 1)
-            push(g, h, 0, first_slot[h], first[h])
-            push(g, h, 0, second_slot[h], second[h])
+            if plane_first[g]:
+                push(g, h, 0, second_slot[h], second[h])
+            else:
+                push(g, h, 1, first_slot[h] + 1, first[h], 3)
+                push(g, h, 1, second_slot[h] + 1, second[h], 3)
             push(g, h, 0, 16, to_core)
 
     def gather_far(g):
         for h in (0, 1):
             slot = first_slot[h]
-            arrived(g, h, slot)
+            if plane_first[g]:
+                for dz in (1, 3, 2):
+                    arrived(g, h, slot + dz, 1)
+            else:
+                arrived(g, h, slot, 1)
+                arrived(g, h, slot + 1, 3)
             push(g, h, slot, 12, second[h])
             push(g, h, slot, 16 + slot, to_core)
 
     def gather_core(g):
         for h in (0, 1):
             slot = second_slot[h]
-            arrived(g, h, slot)
+            if plane_first[g]:
+                arrived(g, h, slot)
+            else:
+                arrived(g, h, slot, 1)
+                arrived(g, h, slot + 1, 3)
             push(g, h, slot, 16 + slot, to_core)
         for h in (0, 1):
             arrived(g, h, 12)
@@ -333,19 +360,37 @@
 
     def scatter_near(g):
         for h in (0, 1):
+            slot = first_slot[h]
             took(g, h, 20)
-            add(g, h, first_slot[h], 20)
-            give(g, h, first_slot[h], 24, first[h])
+            add(g, h, slot, 20)
+            if plane_first[g]:
+                for dz in (2, 3, 1):
+                    give(g, h, slot + dz, 24 + dz, to_z[dz], 1)
+            else:
+                give(g, h, slot, 24, first[h])
 
     def scatter_z(g):
         for h in (0, 1):
             took(g, h, 16)
             add(g, h, 0, 16)
-        for h in (0, 1):
-            took(g, h, 24)
-            add(g, h, 0, 24)
-            for dz in (2, 3, 1):
-                give(g, h, dz, 28 + dz, to_z[dz], 1)
+            if plane_first[g]:
+                for dz in (2, 3, 1):
+                    give(g, h, dz, 28 + dz, to_z[dz], 1)
+        for h in (0, 1):
+            if plane_first[g]:
+                slot = first_slot[h]
+                for dz in (1, 3, 2):
+                    took(g, h, 24 + dz, 1)
+                total = partial[h][g, slot].astype(jnp.float32)
+                for dz in (1, 3, 2):
+                    total = total + landing[h][g, 24 + dz].astype(jnp.float32)
+                partial[h][g, slot] = total.astype(jnp.bfloat16)
+                give(g, h, slot, 24, first[h], 1)
+            else:
+                took(g, h, 24)
+                add(g, h, 0, 24)
+                for dz in (2, 3, 1):
+                    give(g, h, dz, 28 + dz, to_z[dz], 1)
 
     totals = ([], [])
 
@@ -355,10 +400,34 @@
             for dz in (1, 3, 2):
                 took(g, h, 28 + dz, 1)
                 total = total + landing[h][g, 28 + dz].astype(jnp.float32)
+            if plane_first[g]:
+                took(g, h, 24, 1)
+                total = total + landing[h][g, 24].astype(jnp.float32)
             totals[h].append(total)
 
-    for g in range(batches):
-        gather_z(g)
+    tiles = half // 128
+
+    def weight_out(lower, upper, more):
+        part = pl.ds(lower * chunk, (upper - lower) * chunk)
+        value = dot_tn(hidden_buf[part, :], cot_buf[part, :])
+        grad_out_ref[...] = grad_out_ref[...] + value if more else value
+
+    def weight_in(lower, upper, more):
+        part = pl.ds(lower * chunk, (upper - lower) * chunk)
+        value = dot_tn(rows_buf[part, :], pre_buf[part, :])
+        for tile in range(tiles):
+            for side in range(2):
+                left = side * half + tile * 128
+                where = pl.ds(tile * 2 + side, width, stride=2 * tiles)
+                piece = value[:, left : left + 128]
+                grad_in_ref[where, :] = grad_in_ref[where, :] + piece if more else piece
+
+    gather_z(0)
+    gather_own(1)
+    gather_own(0)
+    gather_z(1)
+    gather_own(2)
+    gather_z(2)
     gather_plane(0)
     gather_plane(1)
     gather_far(0)
@@ -377,24 +446,19 @@
     gather_core(2)
     scatter_near(0)
     scatter_plane(1)
+    weight_out(0, 2, False)
+    weight_in(0, 2, False)
     gather_end(2)
     compute(2)
     scatter_z(0)
     scatter_near(1)
     scatter_plane(2)
-    grad_out_ref[...] = dot_tn(hidden_buf[...], cot_buf[...])
+    weight_out(2, 3, True)
     save_out = pltpu.make_async_copy(grad_out_ref, grad_out_hbm, local_sem.at[1])
     save_out.start()
+    scatter_near(2)
     scatter_z(1)
-    scatter_near(2)
-    tiles = half // 128
-    grad_in = dot_tn(rows_buf[...], pre_buf[...])
-    for tile in range(tiles):
-        for side in range(2):
-            left = side * half + tile * 128
-            grad_in_ref[pl.ds(tile * 2 + side, width, stride=2 * tiles), :] = grad_in[
-                :, left : left + 128
-            ]
+    weight_in(2, 3, True)
     save_in = pltpu.make_async_copy(grad_in_ref, grad_in_hbm, local_sem.at[0])
     save_in.start()
     scatter_z(2)

time: 60.6 us -> 59.5 us (0.982)
  Pallas kernels: 54.1 us -> 53 us
    pallas_call x1, Pallas kernels: 54.1 us -> 53 us  [dense_plan(): pl.pallas_call(functools.partial(moe_kernel, groups), out_shape=(jax.Shap...]
where the time goes in v4:
time: 59.5 us; the launch traced here: 59.4 us
  Pallas kernels  53 us (89%)
  local copies, waits for them, and re-layouts  5.64 us (9%)
  between operations  0.73 us (1%)
    pallas_call x1, Pallas kernels, dense_plan(): pl.pallas_call(functools.partial(moe_kernel, groups), out_shape=(jax.Shap...  53 us
    unnamed x16, local copies, waits for them, and re-layouts  5.64 us

profile of v4, /device:TPU:0, one launch (start us, length us, event | category | flops | bytes accessed | tf_op | source)
XLA Modules:
  0.0 59.4 jit_solution(329853465128977091)
XLA Ops:
  0.6 0.0 copy-start
  0.6 0.0 copy-start.4
  0.7 0.0 copy-start.3
  0.7 0.0 copy-start.2
  0.7 0.0 copy-start.1
  0.7 1.5 %copy.12 = bf16[128,8,2,256]{3,1,2,0:T(8,128)(2,1)S(1)} copy(bf16[128,8,2,256]{3,2,1,0:T(2,128)(2,1)} %bitcast.20) | data formatting | bytes 2097152
  2.2 0.0 copy-done
  2.2 0.0 copy-done.4
  2.2 0.0 copy-done.3
  2.2 0.0 copy-done.2
  2.2 0.0 copy-done.1
  2.2 53.0 %shard_map.101 = (bf16[24,1024]{1,0:T(8,128)(2,1)S(1)}, bf16[24,1024]{1,0:T(8,128)(2,1)S(1)}, f32[8,24]{1,0:T(8,128)S(1)}, f32[4096,128]{1,0:T(8,128)S(1)}, f32[256,1024]{1,0:T(8,128)S(1)}) custom-call(bf16[24,1024]{1,0:T(8,128)(2,1)S(1)} %copy-done.1, bf16[24,1024]{1,0:T(8,128)(2,1)S(1)} %copy-done.2, s32[8,24]{1,0:T(8,128)S(1)} %bitcast.18, ...), custom_call_target="tpu_custom_call" | custom-call | flops 3623878656 | bytes 4718592 | tf_op jit(solution)/shard_map/pallas_call | solution.py:495
  55.2 0.6 %copy.18 = bf16[24,1024]{1,0:T(8,128)(2,1)} copy(bf16[24,1024]{1,0:T(8,128)(2,1)S(1)} %get-tuple-element.20) | data formatting | bytes 98304
  55.9 0.6 %copy.19 = bf16[24,1024]{1,0:T(8,128)(2,1)} copy(bf16[24,1024]{1,0:T(8,128)(2,1)S(1)} %get-tuple-element.21) | data formatting | bytes 98304
  56.5 0.6 copy.20
  57.1 1.3 %copy.21 = f32[1,1024,2,256]{3,2,1,0:T(2,128)} copy(f32[1,1024,2,256]{3,2,1,0:T(2,128)S(1)} %bitcast.13) | data formatting | bytes 4194304
  58.4 1.0 %copy.22 = f32[1,256,1024]{2,1,0:T(8,128)} copy(f32[1,256,1024]{2,1,0:T(8,128)S(1)} %bitcast.14) | data formatting | bytes 2097152
Async XLA Ops:
  0.6 1.6 %copy-start = (bf16[1,256,1024]{2,1,0:T(8,128)(2,1)S(1)}, bf16[1,256,1024]{2,1,0:T(8,128)(2,1)}, u32[]{:S(2)}) copy-start(bf16[1,256,1024]{2,1,0:T(8,128)(2,1)} %param.11) | copy-start | bytes 1572868
  0.6 1.6 %copy-start.4 = (f32[24,8]{0,1:T(8,128)S(1)}, f32[24,8]{0,1:T(8,128)}, u32[]{:S(2)}) copy-start(f32[24,8]{0,1:T(8,128)} %param.9) | copy-start | bytes 2308
  0.7 1.6 %copy-start.3 = (s32[24,8]{0,1:T(8,128)S(1)}, s32[24,8]{0,1:T(8,128)}, u32[]{:S(2)}) copy-start(s32[24,8]{0,1:T(8,128)} %param.8) | copy-start | bytes 2308
  0.7 1.6 %copy-start.2 = (bf16[24,1024]{1,0:T(8,128)(2,1)S(1)}, bf16[24,1024]{1,0:T(8,128)(2,1)}, u32[]{:S(2)}) copy-start(bf16[24,1024]{1,0:T(8,128)(2,1)} %cot_ref.1) | copy-start | bytes 147460
  0.7 1.6 %copy-start.1 = (bf16[24,1024]{1,0:T(8,128)(2,1)S(1)}, bf16[24,1024]{1,0:T(8,128)(2,1)}, u32[]{:S(2)}) copy-start(bf16[24,1024]{1,0:T(8,128)(2,1)} %tokens_ref.1) | copy-start | bytes 147460

commit v5 on v4

--- a/solution.py
+++ b/solution.py
@@ -122,10 +122,6 @@
 GATE_COLS = 128
 
 
-def dot_nt(a, b):
-    return lax.dot_general(a, b, (((1,), (1,)), ((), ())), preferred_element_type=jnp.float32)
-
-
 def dot_tn(a, b):
     return lax.dot_general(a, b, (((0,), (0,)), ((), ())), preferred_element_type=jnp.float32)
 
@@ -134,7 +130,8 @@
     groups, tokens_ref, cot_ref, ids_ref, gates_ref, w_in_hbm, w_out_hbm,
     mixed_ref, grad_tok_ref, grad_gates_ref, grad_in_hbm, grad_out_hbm,
     tok_all, cot_all, part_mixed, part_grad, recv_mixed, recv_grad,
-    rows_buf, cot_buf, hidden_buf, pre_buf, w_in_ref, w_out_ref, grad_in_ref, grad_out_ref,
+    rows_buf, cot_buf, hidden_buf, pre_buf, w_in_ref, w_out_ref, w_in_t, w_out_t,
+    grad_in_ref, grad_out_ref,
     gather_send, gather_recv, scatter_send, scatter_recv, local_sem,
 ):
     count, width = tokens_ref.shape
@@ -323,7 +320,7 @@
         sig = jax.nn.sigmoid(gate_part)
         activated = gate_part * sig
         hidden = activated * up_part
-        back = dot_nt(cot, w_out_ref[...])
+        back = jnp.dot(cot, w_out_t[...], preferred_element_type=jnp.float32)
         gate_grad = jnp.sum(hidden * back, axis=1, keepdims=True)
         gated_hidden = (gate * hidden).astype(jnp.bfloat16)
         gated_back = gate * back
@@ -342,7 +339,7 @@
             jnp.bfloat16
         )
         give(g, 0, 16, 0, to_core, 16)
-        grad_rows = dot_nt(grad_pre, w_in_ref[...])
+        grad_rows = jnp.dot(grad_pre, w_in_t[...], preferred_element_type=jnp.float32)
         part_grad[g] = grad_rows.reshape(blocks, batch, width).astype(jnp.bfloat16)
         give(g, 1, 16, 0, to_core, 16)
 
@@ -428,15 +425,17 @@
     gather_z(1)
     gather_own(2)
     gather_z(2)
+    load_out.wait()
+    w_out_t[...] = w_out_ref[...].T
     gather_plane(0)
+    load_in.wait()
+    w_in_t[...] = w_in_ref[...].T
     gather_plane(1)
     gather_far(0)
     gather_plane(2)
     gather_core(0)
     gather_far(1)
     gather_end(0)
-    load_in.wait()
-    load_out.wait()
     compute(0)
     gather_core(1)
     gather_far(2)
@@ -462,7 +461,11 @@
     save_in = pltpu.make_async_copy(grad_in_ref, grad_in_hbm, local_sem.at[0])
     save_in.start()
     scatter_z(2)
+    last = len(sent) - 6
     for g in range(batches):
+        if g == batches - 1:
+            for copy in sent[:last]:
+                copy.wait_send()
         scatter_end(g)
     total_mixed = jnp.concatenate(totals[0], axis=0)
     mixed_ref[...] = total_mixed[:, :width].astype(jnp.bfloat16)
@@ -476,7 +479,7 @@
     grad_gates_ref[...] = jnp.concatenate(lines, axis=0)
     save_out.wait()
     save_in.wait()
-    for copy in sent:
+    for copy in sent[last:]:
         copy.wait_send()
 
 
@@ -516,6 +519,8 @@
             pltpu.VMEM((total_rows, 2 * half), jnp.bfloat16),
             pltpu.VMEM((width, 2 * half), jnp.bfloat16),
             pltpu.VMEM((half, width), jnp.bfloat16),
+            pltpu.VMEM((2 * half, width), jnp.bfloat16),
+            pltpu.VMEM((width, half), jnp.bfloat16),
             pltpu.VMEM((width * 2 * tiles, 128), jnp.float32),
             pltpu.VMEM((half, width), jnp.float32),
             pltpu.SemaphoreType.DMA((batches, 2, devices)),

time: 59.5 us -> 59.2 us (level)
  no operation moved by 1% of the time
where the time goes in v5:
time: 59.2 us; the launch traced here: 59.1 us
  Pallas kernels  52.7 us (89%)
  local copies, waits for them, and re-layouts  5.64 us (10%)
  between operations  0.73 us (1%)
    pallas_call x1, Pallas kernels, dense_plan(): pl.pallas_call(functools.partial(moe_kernel, groups), out_shape=(jax.Shap...  52.7 us
    unnamed x16, local copies, waits for them, and re-layouts  5.64 us

profile of v5, /device:TPU:0, one launch (start us, length us, event | category | flops | bytes accessed | tf_op | source)
XLA Modules:
  0.0 59.1 jit_solution(453761191706736758)
XLA Ops:
  0.6 0.0 copy-start
  0.6 0.0 copy-start.4
  0.7 0.0 copy-start.3
  0.7 0.0 copy-start.2
  0.7 0.0 copy-start.1
  0.7 1.5 %copy.12 = bf16[128,8,2,256]{3,1,2,0:T(8,128)(2,1)S(1)} copy(bf16[128,8,2,256]{3,2,1,0:T(2,128)(2,1)} %bitcast.20) | data formatting | bytes 2097152
  2.2 0.0 copy-done
  2.2 0.0 copy-done.4
  2.2 0.0 copy-done.3
  2.2 0.0 copy-done.2
  2.2 0.0 copy-done.1
  2.2 52.7 %shard_map.101 = (bf16[24,1024]{1,0:T(8,128)(2,1)S(1)}, bf16[24,1024]{1,0:T(8,128)(2,1)S(1)}, f32[8,24]{1,0:T(8,128)S(1)}, f32[4096,128]{1,0:T(8,128)S(1)}, f32[256,1024]{1,0:T(8,128)S(1)}) custom-call(bf16[24,1024]{1,0:T(8,128)(2,1)S(1)} %copy-done.1, bf16[24,1024]{1,0:T(8,128)(2,1)S(1)} %copy-done.2, s32[8,24]{1,0:T(8,128)S(1)} %bitcast.18, ...), custom_call_target="tpu_custom_call" | custom-call | flops 3623878656 | bytes 4718592 | tf_op jit(solution)/shard_map/pallas_call | solution.py:498
  55.0 0.6 %copy.18 = bf16[24,1024]{1,0:T(8,128)(2,1)} copy(bf16[24,1024]{1,0:T(8,128)(2,1)S(1)} %get-tuple-element.20) | data formatting | bytes 98304
  55.6 0.6 %copy.19 = bf16[24,1024]{1,0:T(8,128)(2,1)} copy(bf16[24,1024]{1,0:T(8,128)(2,1)S(1)} %get-tuple-element.21) | data formatting | bytes 98304
  56.2 0.6 %copy.20 = f32[24,8]{0,1:T(8,128)} copy(f32[24,8]{0,1:T(8,128)S(1)} %bitcast.16) | data formatting | bytes 1536
  56.8 1.3 %copy.21 = f32[1,1024,2,256]{3,2,1,0:T(2,128)} copy(f32[1,1024,2,256]{3,2,1,0:T(2,128)S(1)} %bitcast.13) | data formatting | bytes 4194304
  58.1 1.0 %copy.22 = f32[1,256,1024]{2,1,0:T(8,128)} copy(f32[1,256,1024]{2,1,0:T(8,128)S(1)} %bitcast.14) | data formatting | bytes 2097152
Async XLA Ops:
  0.6 1.6 %copy-start = (bf16[1,256,1024]{2,1,0:T(8,128)(2,1)S(1)}, bf16[1,256,1024]{2,1,0:T(8,128)(2,1)}, u32[]{:S(2)}) copy-start(bf16[1,256,1024]{2,1,0:T(8,128)(2,1)} %param.11) | copy-start | bytes 1572868
  0.6 1.6 %copy-start.4 = (f32[24,8]{0,1:T(8,128)S(1)}, f32[24,8]{0,1:T(8,128)}, u32[]{:S(2)}) copy-start(f32[24,8]{0,1:T(8,128)} %param.9) | copy-start | bytes 2308
  0.7 1.6 %copy-start.3 = (s32[24,8]{0,1:T(8,128)S(1)}, s32[24,8]{0,1:T(8,128)}, u32[]{:S(2)}) copy-start(s32[24,8]{0,1:T(8,128)} %param.8) | copy-start | bytes 2308
  0.7 1.6 %copy-start.2 = (bf16[24,1024]{1,0:T(8,128)(2,1)S(1)}, bf16[24,1024]{1,0:T(8,128)(2,1)}, u32[]{:S(2)}) copy-start(bf16[24,1024]{1,0:T(8,128)(2,1)} %cot_ref.1) | copy-start | bytes 147460
  0.7 1.6 %copy-start.1 = (bf16[24,1024]{1,0:T(8,128)(2,1)S(1)}, bf16[24,1024]{1,0:T(8,128)(2,1)}, u32[]{:S(2)}) copy-start(bf16[24,1024]{1,0:T(8,128)(2,1)} %tokens_ref.1) | copy-start | bytes 147460

commit v6 on v5

--- a/solution.py
+++ b/solution.py
@@ -131,12 +131,12 @@
     mixed_ref, grad_tok_ref, grad_gates_ref, grad_in_hbm, grad_out_hbm,
     tok_all, cot_all, part_mixed, part_grad, recv_mixed, recv_grad,
     rows_buf, cot_buf, hidden_buf, pre_buf, w_in_ref, w_out_ref, w_in_t, w_out_t,
-    grad_in_ref, grad_out_ref,
-    gather_send, gather_recv, scatter_send, scatter_recv, local_sem,
+    grad_in_ref, grad_out_ref, their_in, their_out, give_in, give_out, take_in, take_out,
+    gather_send, gather_recv, scatter_send, scatter_recv, local_sem, core_send, core_recv,
 ):
     count, width = tokens_ref.shape
     per_token = ids_ref.shape[0]
-    half = w_out_ref.shape[0]
+    half = w_out_ref.shape[1]
     batches, blocks, batch = tok_all.shape[:3]
     chunk = blocks * batch
     x = lax.axis_index("dp")
@@ -159,8 +159,8 @@
     barrier = pltpu.get_barrier_semaphore()
     for partner in partners:
         pl.semaphore_signal(barrier, inc=1, device_id=partner, device_id_type=MESH)
-    load_in = pltpu.make_async_copy(w_in_hbm, w_in_ref, local_sem.at[0])
-    load_out = pltpu.make_async_copy(w_out_hbm, w_out_ref, local_sem.at[1])
+    load_in = pltpu.make_async_copy(w_in_hbm, w_in_ref.at[0], local_sem.at[0])
+    load_out = pltpu.make_async_copy(w_out_hbm, w_out_ref.at[0], local_sem.at[1])
     load_in.start()
     load_out.start()
 
@@ -196,6 +196,21 @@
         cot_all[g, 0] = own_cot[part].astype(jnp.bfloat16)
     pl.semaphore_wait(barrier, len(partners))
 
+    def swap(src, dst, index):
+        copy = pltpu.make_async_remote_copy(
+            src_ref=src,
+            dst_ref=dst,
+            send_sem=core_send.at[index],
+            recv_sem=core_recv.at[index],
+            device_id=to_core,
+            device_id_type=MESH,
+        )
+        copy.start()
+        return copy
+
+    swap_out = swap(w_out_hbm, w_out_ref.at[1], 0)
+    swap_in = swap(w_in_hbm, w_in_ref.at[1], 1)
+
     gathered = (tok_all, cot_all)
     partial = (part_mixed, part_grad)
     landing = (recv_mixed, recv_grad)
@@ -271,7 +286,6 @@
             else:
                 push(g, h, 1, first_slot[h] + 1, first[h], 3)
                 push(g, h, 1, second_slot[h] + 1, second[h], 3)
-            push(g, h, 0, 16, to_core)
 
     def gather_far(g):
         for h in (0, 1):
@@ -283,9 +297,8 @@
                 arrived(g, h, slot, 1)
                 arrived(g, h, slot + 1, 3)
             push(g, h, slot, 12, second[h])
-            push(g, h, slot, 16 + slot, to_core)
-
-    def gather_core(g):
+
+    def gather_end(g):
         for h in (0, 1):
             slot = second_slot[h]
             if plane_first[g]:
@@ -293,15 +306,7 @@
             else:
                 arrived(g, h, slot, 1)
                 arrived(g, h, slot + 1, 3)
-            push(g, h, slot, 16 + slot, to_core)
-        for h in (0, 1):
             arrived(g, h, 12)
-            push(g, h, 12, 28, to_core)
-
-    def gather_end(g):
-        for slot in (16, 20, 24, 28):
-            for h in (0, 1):
-                arrived(g, h, slot)
 
     wide_col = lax.broadcasted_iota(jnp.int32, (chunk, GATE_COLS), 1)
 
@@ -310,50 +315,52 @@
         packed = tok_all[g].astype(jnp.float32).reshape(chunk, width + GATE_COLS)
         rows = packed[:, :width].astype(jnp.bfloat16)
         cot = cot_all[g].astype(jnp.float32).reshape(chunk, width).astype(jnp.bfloat16)
-        own = jnp.logical_and(wide_col % groups == e, wide_col < 3 * groups)
-        gate = jnp.sum(jnp.where(own, packed[:, width:], 0.0), axis=1, keepdims=True)
         rows_buf[here, :] = rows
         cot_buf[here, :] = cot
-        preact = jnp.dot(rows, w_in_ref[...], preferred_element_type=jnp.float32)
-        gate_part = preact[:, :half]
-        up_part = preact[:, half:]
-        sig = jax.nn.sigmoid(gate_part)
-        activated = gate_part * sig
-        hidden = activated * up_part
-        back = jnp.dot(cot, w_out_t[...], preferred_element_type=jnp.float32)
-        gate_grad = jnp.sum(hidden * back, axis=1, keepdims=True)
-        gated_hidden = (gate * hidden).astype(jnp.bfloat16)
-        gated_back = gate * back
-        grad_gate = gated_back * up_part * (sig * (1.0 + gate_part * (1.0 - sig)))
-        grad_up = gated_back * activated
-        grad_pre = jnp.concatenate([grad_gate, grad_up], axis=1).astype(jnp.bfloat16)
-        hidden_buf[here, :] = gated_hidden
-        pre_buf[here, :] = grad_pre
-        mixed = jnp.dot(gated_hidden, w_out_ref[...], preferred_element_type=jnp.float32)
+        mixed = jnp.zeros((chunk, width), jnp.float32)
+        grad_rows = jnp.zeros((chunk, width), jnp.float32)
+        spread = jnp.zeros((chunk, GATE_COLS), jnp.float32)
+        for side, expert in ((0, e), (1, e + 1 - 2 * c)):
+            own = jnp.logical_and(wide_col % groups == expert, wide_col < 3 * groups)
+            gate = jnp.sum(jnp.where(own, packed[:, width:], 0.0), axis=1, keepdims=True)
+            preact = jnp.dot(rows, w_in_ref[side], preferred_element_type=jnp.float32)
+            gate_part = preact[:, :half]
+            up_part = preact[:, half:]
+            sig = jax.nn.sigmoid(gate_part)
+            activated = gate_part * sig
+            hidden = activated * up_part
+            back = jnp.dot(cot, w_out_t[side], preferred_element_type=jnp.float32)
+            gate_grad = jnp.sum(hidden * back, axis=1, keepdims=True)
+            gated_hidden = (gate * hidden).astype(jnp.bfloat16)
+            gated_back = gate * back
+            grad_gate = gated_back * up_part * (sig * (1.0 + gate_part * (1.0 - sig)))
+            grad_up = gated_back * activated
+            grad_pre = jnp.concatenate([grad_gate, grad_up], axis=1).astype(jnp.bfloat16)
+            hidden_buf[side, here, :] = gated_hidden
+            pre_buf[side, here, :] = grad_pre
+            mixed = mixed + jnp.dot(
+                gated_hidden, w_out_ref[side], preferred_element_type=jnp.float32
+            )
+            grad_rows = grad_rows + jnp.dot(
+                grad_pre, w_in_t[side], preferred_element_type=jnp.float32
+            )
+            high = gate_grad.astype(jnp.bfloat16).astype(jnp.float32)
+            spread = spread + jnp.where(
+                wide_col == expert,
+                high,
+                jnp.where(wide_col == groups + expert, gate_grad - high, 0.0),
+            )
         part_mixed[g, :, :, :width] = mixed.reshape(blocks, batch, width).astype(jnp.bfloat16)
-        high = gate_grad.astype(jnp.bfloat16).astype(jnp.float32)
-        spread = jnp.where(
-            wide_col == e, high, jnp.where(wide_col == groups + e, gate_grad - high, 0.0)
-        )
         part_mixed[g, :, :, width:] = spread.reshape(blocks, batch, GATE_COLS).astype(
             jnp.bfloat16
         )
-        give(g, 0, 16, 0, to_core, 16)
-        grad_rows = jnp.dot(grad_pre, w_in_t[...], preferred_element_type=jnp.float32)
         part_grad[g] = grad_rows.reshape(blocks, batch, width).astype(jnp.bfloat16)
-        give(g, 1, 16, 0, to_core, 16)
 
     def scatter_plane(g):
         for h in (0, 1):
-            took(g, h, 0, 16)
-            add(g, h, 12, 12)
             give(g, h, 12, 20, second[h])
         for h in (0, 1):
-            add(g, h, second_slot[h], second_slot[h])
             give(g, h, second_slot[h], 16, second[h])
-        for h in (0, 1):
-            add(g, h, first_slot[h], first_slot[h])
-            add(g, h, 0, 0)
 
     def scatter_near(g):
         for h in (0, 1):
@@ -406,18 +413,35 @@
 
     def weight_out(lower, upper, more):
         part = pl.ds(lower * chunk, (upper - lower) * chunk)
-        value = dot_tn(hidden_buf[part, :], cot_buf[part, :])
+        value = dot_tn(hidden_buf[0, part, :], cot_buf[part, :])
         grad_out_ref[...] = grad_out_ref[...] + value if more else value
 
     def weight_in(lower, upper, more):
         part = pl.ds(lower * chunk, (upper - lower) * chunk)
-        value = dot_tn(rows_buf[part, :], pre_buf[part, :])
+        value = dot_tn(rows_buf[part, :], pre_buf[0, part, :])
         for tile in range(tiles):
             for side in range(2):
                 left = side * half + tile * 128
                 where = pl.ds(tile * 2 + side, width, stride=2 * tiles)
                 piece = value[:, left : left + 128]
                 grad_in_ref[where, :] = grad_in_ref[where, :] + piece if more else piece
+
+    def their_weights(lower, upper, more):
+        part = pl.ds(lower * chunk, (upper - lower) * chunk)
+        value = dot_tn(hidden_buf[1, part, :], cot_buf[part, :])
+        if more:
+            give_out[...] = (their_out[...] + value).astype(jnp.bfloat16)
+            swaps.append(swap(give_out, take_out, 2))
+        else:
+            their_out[...] = value
+        value = dot_tn(rows_buf[part, :], pre_buf[1, part, :])
+        if more:
+            give_in[...] = (their_in[...] + value).astype(jnp.bfloat16)
+            swaps.append(swap(give_in, take_in, 3))
+        else:
+            their_in[...] = value
+
+    swaps = [swap_out, swap_in]
 
     gather_z(0)
     gather_own(1)
@@ -426,41 +450,54 @@
     gather_own(2)
     gather_z(2)
     load_out.wait()
-    w_out_t[...] = w_out_ref[...].T
+    w_out_t[0] = w_out_ref[0].T
     gather_plane(0)
     load_in.wait()
-    w_in_t[...] = w_in_ref[...].T
+    w_in_t[0] = w_in_ref[0].T
     gather_plane(1)
     gather_far(0)
     gather_plane(2)
-    gather_core(0)
+    swap_out.wait_recv()
+    w_out_t[1] = w_out_ref[1].T
+    swap_in.wait_recv()
+    w_in_t[1] = w_in_ref[1].T
     gather_far(1)
     gather_end(0)
     compute(0)
-    gather_core(1)
+    scatter_plane(0)
     gather_far(2)
-    scatter_plane(0)
     gather_end(1)
     compute(1)
-    gather_core(2)
+    scatter_plane(1)
     scatter_near(0)
-    scatter_plane(1)
+    their_weights(0, 2, False)
     weight_out(0, 2, False)
     weight_in(0, 2, False)
     gather_end(2)
     compute(2)
+    scatter_plane(2)
     scatter_z(0)
     scatter_near(1)
-    scatter_plane(2)
+    their_weights(2, 3, True)
+    scatter_near(2)
+    scatter_z(1)
     weight_out(2, 3, True)
+    weight_in(2, 3, True)
+    scatter_z(2)
+    swaps[2].wait_recv()
+    grad_out_ref[...] = grad_out_ref[...] + take_out[...].astype(jnp.float32)
     save_out = pltpu.make_async_copy(grad_out_ref, grad_out_hbm, local_sem.at[1])
     save_out.start()
-    scatter_near(2)
-    scatter_z(1)
-    weight_in(2, 3, True)
+    swaps[3].wait_recv()
+    for tile in range(tiles):
+        for side in range(2):
+            left = side * half + tile * 128
+            where = pl.ds(tile * 2 + side, width, stride=2 * tiles)
+            grad_in_ref[where, :] = grad_in_ref[where, :] + take_in[
+                :, left : left + 128
+            ].astype(jnp.float32)
     save_in = pltpu.make_async_copy(grad_in_ref, grad_in_hbm, local_sem.at[0])
     save_in.start()
-    scatter_z(2)
     last = len(sent) - 6
     for g in range(batches):
         if g == batches - 1:
@@ -479,7 +516,7 @@
     grad_gates_ref[...] = jnp.concatenate(lines, axis=0)
     save_out.wait()
     save_in.wait()
-    for copy in sent[last:]:
+    for copy in swaps + sent[last:]:
         copy.wait_send()
 
 
@@ -507,27 +544,35 @@
         in_specs=[vmem] * 4 + [anywhere] * 2,
         out_specs=[vmem] * 3 + [anywhere] * 2,
         scratch_shapes=[
+            pltpu.VMEM((batches, groups, batch, wide), jnp.bfloat16),
+            pltpu.VMEM((batches, groups, batch, width), jnp.bfloat16),
+            pltpu.VMEM((batches, groups, batch, wide), jnp.bfloat16),
+            pltpu.VMEM((batches, groups, batch, width), jnp.bfloat16),
             pltpu.VMEM((batches, devices, batch, wide), jnp.bfloat16),
             pltpu.VMEM((batches, devices, batch, width), jnp.bfloat16),
-            pltpu.VMEM((batches, devices, batch, wide), jnp.bfloat16),
-            pltpu.VMEM((batches, devices, batch, width), jnp.bfloat16),
-            pltpu.VMEM((batches, devices, batch, wide), jnp.bfloat16),
-            pltpu.VMEM((batches, devices, batch, width), jnp.bfloat16),
-            pltpu.VMEM((total_rows, width), jnp.bfloat16),
-            pltpu.VMEM((total_rows, width), jnp.bfloat16),
-            pltpu.VMEM((total_rows, half), jnp.bfloat16),
-            pltpu.VMEM((total_rows, 2 * half), jnp.bfloat16),
+            pltpu.VMEM((total_rows // 2, width), jnp.bfloat16),
+            pltpu.VMEM((total_rows // 2, width), jnp.bfloat16),
+            pltpu.VMEM((2, total_rows // 2, half), jnp.bfloat16),
+            pltpu.VMEM((2, total_rows // 2, 2 * half), jnp.bfloat16),
+            pltpu.VMEM((2, width, 2 * half), jnp.bfloat16),
+            pltpu.VMEM((2, half, width), jnp.bfloat16),
+            pltpu.VMEM((2, 2 * half, width), jnp.bfloat16),
+            pltpu.VMEM((2, width, half), jnp.bfloat16),
+            pltpu.VMEM((width * 2 * tiles, 128), jnp.float32),
+            pltpu.VMEM((half, width), jnp.float32),
+            pltpu.VMEM((width, 2 * half), jnp.float32),
+            pltpu.VMEM((half, width), jnp.float32),
             pltpu.VMEM((width, 2 * half), jnp.bfloat16),
             pltpu.VMEM((half, width), jnp.bfloat16),
-            pltpu.VMEM((2 * half, width), jnp.bfloat16),
-            pltpu.VMEM((width, half), jnp.bfloat16),
-            pltpu.VMEM((width * 2 * tiles, 128), jnp.float32),
-            pltpu.VMEM((half, width), jnp.float32),
+            pltpu.VMEM((width, 2 * half), jnp.bfloat16),
+            pltpu.VMEM((half, width), jnp.bfloat16),
             pltpu.SemaphoreType.DMA((batches, 2, devices)),
             pltpu.SemaphoreType.DMA((batches, 2, devices)),
             pltpu.SemaphoreType.DMA((batches, 2, devices)),
             pltpu.SemaphoreType.DMA((batches, 2, devices)),
             pltpu.SemaphoreType.DMA((2,)),
+            pltpu.SemaphoreType.DMA((4,)),
+            pltpu.SemaphoreType.DMA((4,)),
         ],
         compiler_params=pltpu.CompilerParams(
             collective_id=0, has_side_effects=True, vmem_limit_bytes=44 * 1024 * 1024

time: 59.2 us -> 58.6 us (0.990)
  Pallas kernels: 52.7 us -> 52.1 us
    pallas_call x1, Pallas kernels: 52.7 us -> 52.1 us  [dense_plan(): pl.pallas_call(functools.partial(moe_kernel, groups), out_shape=(jax.Shap...]
where the time goes in v6:
time: 58.6 us; the launch traced here: 58.4 us
  Pallas kernels  52.1 us (89%)
  local copies, waits for them, and re-layouts  5.64 us (10%)
  between operations  0.73 us (1%)
    pallas_call x1, Pallas kernels, dense_plan(): pl.pallas_call(functools.partial(moe_kernel, groups), out_shape=(jax.Shap...  52.1 us
    unnamed x16, local copies, waits for them, and re-layouts  5.64 us

profile of v6, /device:TPU:0, one launch (start us, length us, event | category | flops | bytes accessed | tf_op | source)
XLA Modules:
  0.0 58.4 jit_solution(10429666865911029856)
XLA Ops:
  0.6 0.0 copy-start
  0.6 0.0 copy-start.4
  0.7 0.0 copy-start.3
  0.7 0.0 copy-start.2
  0.7 0.0 copy-start.1
  0.7 1.5 %copy.12 = bf16[128,8,2,256]{3,1,2,0:T(8,128)(2,1)S(1)} copy(bf16[128,8,2,256]{3,2,1,0:T(2,128)(2,1)} %bitcast.20) | data formatting | bytes 2097152
  2.2 0.0 copy-done
  2.2 0.0 copy-done.4
  2.2 0.0 copy-done.3
  2.2 0.0 copy-done.2
  2.2 0.0 copy-done.1
  2.2 52.1 %shard_map.101 = (bf16[24,1024]{1,0:T(8,128)(2,1)S(1)}, bf16[24,1024]{1,0:T(8,128)(2,1)S(1)}, f32[8,24]{1,0:T(8,128)S(1)}, f32[4096,128]{1,0:T(8,128)S(1)}, f32[256,1024]{1,0:T(8,128)S(1)}) custom-call(bf16[24,1024]{1,0:T(8,128)(2,1)S(1)} %copy-done.1, bf16[24,1024]{1,0:T(8,128)(2,1)S(1)} %copy-done.2, s32[8,24]{1,0:T(8,128)S(1)} %bitcast.18, ...), custom_call_target="tpu_custom_call" | custom-call | flops 3623878656 | bytes 4718592 | tf_op jit(solution)/shard_map/pallas_call | solution.py:535
  54.3 0.6 %copy.18 = bf16[24,1024]{1,0:T(8,128)(2,1)} copy(bf16[24,1024]{1,0:T(8,128)(2,1)S(1)} %get-tuple-element.20) | data formatting | bytes 98304
  54.9 0.6 %copy.19 = bf16[24,1024]{1,0:T(8,128)(2,1)} copy(bf16[24,1024]{1,0:T(8,128)(2,1)S(1)} %get-tuple-element.21) | data formatting | bytes 98304
  55.6 0.6 %copy.20 = f32[24,8]{0,1:T(8,128)} copy(f32[24,8]{0,1:T(8,128)S(1)} %bitcast.16) | data formatting | bytes 1536
  56.1 1.3 %copy.21 = f32[1,1024,2,256]{3,2,1,0:T(2,128)} copy(f32[1,1024,2,256]{3,2,1,0:T(2,128)S(1)} %bitcast.13) | data formatting | bytes 4194304
  57.5 1.0 %copy.22 = f32[1,256,1024]{2,1,0:T(8,128)} copy(f32[1,256,1024]{2,1,0:T(8,128)S(1)} %bitcast.14) | data formatting | bytes 2097152
Async XLA Ops:
  0.6 1.6 %copy-start = (bf16[1,256,1024]{2,1,0:T(8,128)(2,1)S(1)}, bf16[1,256,1024]{2,1,0:T(8,128)(2,1)}, u32[]{:S(2)}) copy-start(bf16[1,256,1024]{2,1,0:T(8,128)(2,1)} %param.11) | copy-start | bytes 1572868
  0.6 1.6 %copy-start.4 = (f32[24,8]{0,1:T(8,128)S(1)}, f32[24,8]{0,1:T(8,128)}, u32[]{:S(2)}) copy-start(f32[24,8]{0,1:T(8,128)} %param.9) | copy-start | bytes 2308
  0.7 1.6 %copy-start.3 = (s32[24,8]{0,1:T(8,128)S(1)}, s32[24,8]{0,1:T(8,128)}, u32[]{:S(2)}) copy-start(s32[24,8]{0,1:T(8,128)} %param.8) | copy-start | bytes 2308
  0.7 1.6 %copy-start.2 = (bf16[24,1024]{1,0:T(8,128)(2,1)S(1)}, bf16[24,1024]{1,0:T(8,128)(2,1)}, u32[]{:S(2)}) copy-start(bf16[24,1024]{1,0:T(8,128)(2,1)} %cot_ref.1) | copy-start | bytes 147460
  0.7 1.6 %copy-start.1 = (bf16[24,1024]{1,0:T(8,128)(2,1)S(1)}, bf16[24,1024]{1,0:T(8,128)(2,1)}, u32[]{:S(2)}) copy-start(bf16[24,1024]{1,0:T(8,128)(2,1)} %tokens_ref.1) | copy-start | bytes 147460

commit v7 on v6

--- a/solution.py
+++ b/solution.py
@@ -128,10 +128,10 @@
 
 def moe_kernel(
     groups, tokens_ref, cot_ref, ids_ref, gates_ref, w_in_hbm, w_out_hbm,
-    mixed_ref, grad_tok_ref, grad_gates_ref, grad_in_hbm, grad_out_hbm,
+    mixed_ref, grad_tok_ref, grad_gates_ref, grad_in_ref, grad_out_ref,
     tok_all, cot_all, part_mixed, part_grad, recv_mixed, recv_grad,
     rows_buf, cot_buf, hidden_buf, pre_buf, w_in_ref, w_out_ref, w_in_t, w_out_t,
-    grad_in_ref, grad_out_ref, their_in, their_out, give_in, give_out, take_in, take_out,
+    give_in, give_out, take_in, take_out,
     gather_send, gather_recv, scatter_send, scatter_recv, local_sem, core_send, core_recv,
 ):
     count, width = tokens_ref.shape
@@ -411,35 +411,20 @@
 
     tiles = half // 128
 
-    def weight_out(lower, upper, more):
-        part = pl.ds(lower * chunk, (upper - lower) * chunk)
-        value = dot_tn(hidden_buf[0, part, :], cot_buf[part, :])
-        grad_out_ref[...] = grad_out_ref[...] + value if more else value
-
-    def weight_in(lower, upper, more):
-        part = pl.ds(lower * chunk, (upper - lower) * chunk)
-        value = dot_tn(rows_buf[part, :], pre_buf[0, part, :])
+    def own_weights():
+        grad_out_ref[...] = dot_tn(hidden_buf[0], cot_buf[...])
+        value = dot_tn(rows_buf[...], pre_buf[0])
         for tile in range(tiles):
             for side in range(2):
                 left = side * half + tile * 128
                 where = pl.ds(tile * 2 + side, width, stride=2 * tiles)
-                piece = value[:, left : left + 128]
-                grad_in_ref[where, :] = grad_in_ref[where, :] + piece if more else piece
-
-    def their_weights(lower, upper, more):
-        part = pl.ds(lower * chunk, (upper - lower) * chunk)
-        value = dot_tn(hidden_buf[1, part, :], cot_buf[part, :])
-        if more:
-            give_out[...] = (their_out[...] + value).astype(jnp.bfloat16)
-            swaps.append(swap(give_out, take_out, 2))
-        else:
-            their_out[...] = value
-        value = dot_tn(rows_buf[part, :], pre_buf[1, part, :])
-        if more:
-            give_in[...] = (their_in[...] + value).astype(jnp.bfloat16)
-            swaps.append(swap(give_in, take_in, 3))
-        else:
-            their_in[...] = value
+                grad_in_ref[where, :] = value[:, left : left + 128]
+
+    def their_weights():
+        give_in[...] = dot_tn(rows_buf[...], pre_buf[1]).astype(jnp.bfloat16)
+        swaps.append(swap(give_in, take_in, 3))
+        give_out[...] = dot_tn(hidden_buf[1], cot_buf[...]).astype(jnp.bfloat16)
+        swaps.append(swap(give_out, take_out, 2))
 
     swaps = [swap_out, swap_in]
 
@@ -470,25 +455,17 @@
     compute(1)
     scatter_plane(1)
     scatter_near(0)
-    their_weights(0, 2, False)
-    weight_out(0, 2, False)
-    weight_in(0, 2, False)
     gather_end(2)
     compute(2)
     scatter_plane(2)
     scatter_z(0)
     scatter_near(1)
-    their_weights(2, 3, True)
+    their_weights()
     scatter_near(2)
     scatter_z(1)
-    weight_out(2, 3, True)
-    weight_in(2, 3, True)
+    own_weights()
     scatter_z(2)
     swaps[2].wait_recv()
-    grad_out_ref[...] = grad_out_ref[...] + take_out[...].astype(jnp.float32)
-    save_out = pltpu.make_async_copy(grad_out_ref, grad_out_hbm, local_sem.at[1])
-    save_out.start()
-    swaps[3].wait_recv()
     for tile in range(tiles):
         for side in range(2):
             left = side * half + tile * 128
@@ -496,8 +473,8 @@
             grad_in_ref[where, :] = grad_in_ref[where, :] + take_in[
                 :, left : left + 128
             ].astype(jnp.float32)
-    save_in = pltpu.make_async_copy(grad_in_ref, grad_in_hbm, local_sem.at[0])
-    save_in.start()
+    swaps[3].wait_recv()
+    grad_out_ref[...] = grad_out_ref[...] + take_out[...].astype(jnp.float32)
     last = len(sent) - 6
     for g in range(batches):
         if g == batches - 1:
@@ -514,8 +491,6 @@
         value = jnp.sum(jnp.where(chosen, by_expert, 0.0), axis=1, keepdims=True)
         lines.append(jnp.sum(jnp.where(diagonal, value, 0.0), axis=0, keepdims=True))
     grad_gates_ref[...] = jnp.concatenate(lines, axis=0)
-    save_out.wait()
-    save_in.wait()
     for copy in swaps + sent[last:]:
         copy.wait_send()
 
@@ -542,7 +517,7 @@
             jax.ShapeDtypeStruct((half, width), jnp.float32),
         ),
         in_specs=[vmem] * 4 + [anywhere] * 2,
-        out_specs=[vmem] * 3 + [anywhere] * 2,
+        out_specs=[vmem] * 5,
         scratch_shapes=[
             pltpu.VMEM((batches, groups, batch, wide), jnp.bfloat16),
             pltpu.VMEM((batches, groups, batch, width), jnp.bfloat16),
@@ -558,10 +533,6 @@
             pltpu.VMEM((2, half, width), jnp.bfloat16),
             pltpu.VMEM((2, 2 * half, width), jnp.bfloat16),
             pltpu.VMEM((2, width, half), jnp.bfloat16),
-            pltpu.VMEM((width * 2 * tiles, 128), jnp.float32),
-            pltpu.VMEM((half, width), jnp.float32),
-            pltpu.VMEM((width, 2 * half), jnp.float32),
-            pltpu.VMEM((half, width), jnp.float32),
             pltpu.VMEM((width, 2 * half), jnp.bfloat16),
             pltpu.VMEM((half, width), jnp.bfloat16),
             pltpu.VMEM((width, 2 * half), jnp.bfloat16),

time: 58.6 us -> 58.8 us (level)
  no operation moved by 1% of the time
where the time goes in v7:
time: 58.8 us; the launch traced here: 58.7 us
  Pallas kernels  52.3 us (89%)
  local copies, waits for them, and re-layouts  5.64 us (10%)
  between operations  0.73 us (1%)
    pallas_call x1, Pallas kernels, dense_plan(): pl.pallas_call(functools.partial(moe_kernel, groups), out_shape=(jax.Shap...  52.3 us
    unnamed x16, local copies, waits for them, and re-layouts  5.64 us

profile of v7, /device:TPU:0, one launch (start us, length us, event | category | flops | bytes accessed | tf_op | source)
XLA Modules:
  0.0 58.7 jit_solution(17924976340060419390)
XLA Ops:
  0.6 0.0 copy-start
  0.6 0.0 copy-start.4
  0.7 0.0 copy-start.3
  0.7 0.0 copy-start.2
  0.7 0.0 copy-start.1
  0.7 1.5 %copy.12 = bf16[128,8,2,256]{3,1,2,0:T(8,128)(2,1)S(1)} copy(bf16[128,8,2,256]{3,2,1,0:T(2,128)(2,1)} %bitcast.20) | data formatting | bytes 2097152
  2.2 0.0 copy-done
  2.2 0.0 copy-done.4
  2.2 0.0 copy-done.3
  2.2 0.0 copy-done.2
  2.2 0.0 copy-done.1
  2.2 52.3 %shard_map.101 = (bf16[24,1024]{1,0:T(8,128)(2,1)S(1)}, bf16[24,1024]{1,0:T(8,128)(2,1)S(1)}, f32[8,24]{1,0:T(8,128)S(1)}, f32[4096,128]{1,0:T(8,128)S(1)}, f32[256,1024]{1,0:T(8,128)S(1)}) custom-call(bf16[24,1024]{1,0:T(8,128)(2,1)S(1)} %copy-done.1, bf16[24,1024]{1,0:T(8,128)(2,1)S(1)} %copy-done.2, s32[8,24]{1,0:T(8,128)S(1)} %bitcast.18, ...), custom_call_target="tpu_custom_call" | custom-call | flops 3623878656 | bytes 4718592 | tf_op jit(solution)/shard_map/pallas_call | solution.py:510
  54.5 0.6 %copy.18 = bf16[24,1024]{1,0:T(8,128)(2,1)} copy(bf16[24,1024]{1,0:T(8,128)(2,1)S(1)} %get-tuple-element.20) | data formatting | bytes 98304
  55.2 0.6 %copy.19 = bf16[24,1024]{1,0:T(8,128)(2,1)} copy(bf16[24,1024]{1,0:T(8,128)(2,1)S(1)} %get-tuple-element.21) | data formatting | bytes 98304
  55.8 0.6 %copy.20 = f32[24,8]{0,1:T(8,128)} copy(f32[24,8]{0,1:T(8,128)S(1)} %bitcast.16) | data formatting | bytes 1536
  56.4 1.3 %copy.21 = f32[1,1024,2,256]{3,2,1,0:T(2,128)} copy(f32[1,1024,2,256]{3,2,1,0:T(2,128)S(1)} %bitcast.13) | data formatting | bytes 4194304
  57.7 1.0 %copy.22 = f32[1,256,1024]{2,1,0:T(8,128)} copy(f32[1,256,1024]{2,1,0:T(8,128)S(1)} %bitcast.14) | data formatting | bytes 2097152
Async XLA Ops:
  0.6 1.6 %copy-start = (bf16[1,256,1024]{2,1,0:T(8,128)(2,1)S(1)}, bf16[1,256,1024]{2,1,0:T(8,128)(2,1)}, u32[]{:S(2)}) copy-start(bf16[1,256,1024]{2,1,0:T(8,128)(2,1)} %param.11) | copy-start | bytes 1572868
  0.6 1.6 %copy-start.4 = (f32[24,8]{0,1:T(8,128)S(1)}, f32[24,8]{0,1:T(8,128)}, u32[]{:S(2)}) copy-start(f32[24,8]{0,1:T(8,128)} %param.9) | copy-start | bytes 2308
  0.7 1.6 %copy-start.3 = (s32[24,8]{0,1:T(8,128)S(1)}, s32[24,8]{0,1:T(8,128)}, u32[]{:S(2)}) copy-start(s32[24,8]{0,1:T(8,128)} %param.8) | copy-start | bytes 2308
  0.7 1.6 %copy-start.2 = (bf16[24,1024]{1,0:T(8,128)(2,1)S(1)}, bf16[24,1024]{1,0:T(8,128)(2,1)}, u32[]{:S(2)}) copy-start(bf16[24,1024]{1,0:T(8,128)(2,1)} %cot_ref.1) | copy-start | bytes 147460
  0.7 1.6 %copy-start.1 = (bf16[24,1024]{1,0:T(8,128)(2,1)S(1)}, bf16[24,1024]{1,0:T(8,128)(2,1)}, u32[]{:S(2)}) copy-start(bf16[24,1024]{1,0:T(8,128)(2,1)} %tokens_ref.1) | copy-start | bytes 147460
